TPU v7x, 32 devices: a whole 2x2x4 slice. The times are simulated.
32 devices in a mesh: groups: 2 (over y), outer: 4 (over x, core), inner: 4 (over z).
Axes of the slice: x: 2, y: 2, z: 4, core: 2. Of those that a mesh axis runs over, the one named last changes fastest.
Arguments:
- activations: bfloat16 [4096, 8192], P(('groups', 'outer', 'inner')), parts along dimension 0, may hold values from -64 to 64
- upstream: bfloat16 [4096, 768], P(('groups', 'outer', 'inner')), parts along dimension 0, may hold values from -8 to 8
- frozen_weight_matrix: bfloat16 [8192, 768], P(('outer', 'inner')), may hold values from -0.21875 to 0.21875
- master: float32 [1146880], P(('groups', 'outer', 'inner')), parts along dimension 0, may hold values from -6 to 6
- moment: float32 [1146880], P(('groups', 'outer', 'inner')), parts along dimension 0, may hold values from -3 to 3
- second_moment: float32 [1146880], P(('groups', 'outer', 'inner')), parts along dimension 0, may hold values from 0.01 to 1
Outputs:
- input_gradient_rows: bfloat16 [4096, 8192], P(('groups', 'outer', 'inner')), parts along dimension 0
- new_master: float32 [1146880], P(('groups', 'outer', 'inner')), parts along dimension 0
- new_moment: float32 [1146880], P(('groups', 'outer', 'inner')), parts along dimension 0
- new_second: float32 [1146880], P(('groups', 'outer', 'inner')), parts along dimension 0
There are 2 independent parts, one for each index of `groups`. A program takes and returns all parts, laid end to end along the dimension named above; an argument that names none is the same for every part. Nothing has to cross between parts.
All inputs are finite; a program needn't handle non-finite values.
Results may differ from a plain program's by a relative error of at most 0.001.
The roundings to bfloat16 on the way count: a program that leaves them out, or rounds other values in their place, can miss the bound.
Values may be sent and summed in bfloat16 or wider, within the bound.
A program may use at most 128 MiB of HBM per device.

v0:
```python
import math

import jax
import jax.numpy as jnp
from jax import lax
from jax.sharding import PartitionSpec as P


def per_device(activations, upstream, frozen_weight_matrix, master, moment, second_moment):
    width = activations.shape[1]
    value_width = upstream.shape[1]
    whole = lax.all_gather(master.astype(jnp.bfloat16), ("outer", "inner"), axis=0, tiled=True)
    rank_activations = whole.shape[0] // (width + value_width)
    adapter_scale_factor = 0.5 / math.sqrt(rank_activations * value_width)
    down_weight_transposed = whole[: rank_activations * width].reshape(rank_activations, width)
    up_m = whole[rank_activations * width :].reshape(rank_activations, value_width)
    rank_gradient = jnp.dot(upstream, up_m.T, preferred_element_type=jnp.float32).astype(
        jnp.bfloat16
    )
    projected_rows = jnp.dot(
        activations, down_weight_transposed.T, preferred_element_type=jnp.float32
    ).astype(jnp.bfloat16)
    down_weight_gradient = adapter_scale_factor * jnp.dot(
        rank_gradient.T, activations, preferred_element_type=jnp.float32
    )
    up_weight_gradient = adapter_scale_factor * jnp.dot(
        projected_rows.T, upstream, preferred_element_type=jnp.float32
    )
    flat_grad = jnp.concatenate([down_weight_gradient.reshape(-1), up_weight_gradient.reshape(-1)])
    grad_shard = lax.psum_scatter(flat_grad, ("outer", "inner"), scatter_dimension=0, tiled=True)
    sum_squares = lax.psum(jnp.sum(grad_shard * grad_shard), ("outer", "inner"))
    feat_rows = frozen_weight_matrix.shape[0]
    feat_start = lax.axis_index(("outer", "inner")) * feat_rows
    own_cols = lax.dynamic_slice_in_dim(down_weight_transposed, feat_start, feat_rows, 1)
    tok_piece = lax.all_gather(upstream, ("outer", "inner"), axis=0, tiled=True)
    rank_piece = jnp.dot(tok_piece, up_m.T, preferred_element_type=jnp.float32).astype(jnp.bfloat16)
    frozen_output = lax.dot_general(
        tok_piece,
        frozen_weight_matrix,
        (((1,), (1,)), ((), ())),
        preferred_element_type=jnp.float32,
    )
    feat_block = (
        frozen_output
        + adapter_scale_factor * jnp.dot(rank_piece, own_cols, preferred_element_type=jnp.float32)
    ).astype(jnp.bfloat16)
    n_outer = lax.axis_size("outer")
    n_inner = lax.axis_size("inner")
    tok_count = upstream.shape[0]
    reordered = (
        feat_block.reshape(n_outer, n_inner, tok_count, feat_rows)
        .transpose(1, 0, 2, 3)
        .reshape(n_inner * n_outer * tok_count, feat_rows)
    )
    input_gradient_rows = lax.all_to_all(
        lax.all_to_all(reordered, "inner", split_axis=0, concat_axis=1, tiled=True),
        "outer",
        split_axis=0,
        concat_axis=1,
        tiled=True,
    )
    norm = jnp.sqrt(sum_squares + 1e-06)
    clipped = grad_shard * jnp.minimum(1.0, math.sqrt(whole.shape[0]) / norm)
    new_moment = 0.9 * moment + 0.1 * clipped
    new_second = 0.999 * second_moment + 0.001 * clipped * clipped
    corr_one = 1.0 - 0.9**10
    corr_two = 1.0 - 0.999**10
    new_master = master - 0.1 * (new_moment / corr_one) / (jnp.sqrt(new_second / corr_two) + 1e-08)
    return (input_gradient_rows, new_master, new_moment, new_second)


def solution(mesh):
    return jax.shard_map(
        per_device,
        mesh=mesh,
        in_specs=(
            P(("groups", "outer", "inner"), None),
            P(("groups", "outer", "inner"), None),
            P(("outer", "inner"), None),
            P(("groups", "outer", "inner")),
            P(("groups", "outer", "inner")),
            P(("groups", "outer", "inner")),
        ),
        out_specs=(
            P(("groups", "outer", "inner"), None),
            P(("groups", "outer", "inner")),
            P(("groups", "outer", "inner")),
            P(("groups", "outer", "inner")),
        ),
        check_vma=False,
    )
```

profile of v0, /device:TPU:0, one launch (start us, length us, event | category | flops | bytes accessed | tf_op | source)
XLA Modules:
  0.0 299.8 jit_solution(9990898749863622905)
XLA Ops:
  7.2 1.7 convert_element_type.15
  9.7 42.1 %all-gather.5.cloned.1.call-done = bf16[573440]{0:T(1024)(128)(2,1)} async-done(((bf16[35840]{0:T(1024)(128)(2,1)}), bf16[573440]{0:T(1024)(128)(2,1)}) %all-gather.5.cloned.1.call-update) | async-done | bytes 1146896 | tf_op jit(solution)/shard_map/all_gather | solution.py:12
  51.8 2.3 slice.20
  54.1 1.5 slice.18
  55.8 2.0 fusion
  57.8 3.4 %copy.20 = f32[8,64,8,128]{3,1,2,0:T(8,128)} copy(f32[8,64,8,128]{3,2,1,0:T(8,128)} %fusion) | data formatting | bytes 4194304
  61.2 1.7 convolution_multiply_fusion.1
  62.9 0.9 reshape.41
  63.8 34.5 %all-gather.3.cloned.1.call-done = bf16[2048,768]{1,0:T(8,128)(2,1)} async-done(((bf16[128,768]{1,0:T(8,128)(2,1)}), bf16[2048,768]{1,0:T(8,128)(2,1)}) %all-gather.3.cloned.1.call-update) | async-done | bytes 3145744 | tf_op jit(solution)/shard_map/all_gather | solution.py:35
  98.3 5.9 %fusion.5 = f32[2048,512]{1,0:T(8,128)} fusion(bf16[2048,768]{1,0:T(8,128)(2,1)} %all-gather.3.cloned.1.call-done, bf16[512,768]{1,0:T(8,128)(2,1)} %param.8), kind=kOutput, calls=%fused_computation.15 | convolution fusion | flops 1610612736 | bytes 8126464 | tf_op jit(solution)/shard_map/dot_general | solution.py:37
  104.2 6.1 %add_convert_fusion = bf16[2048,512]{1,0:T(8,128)(2,1)} fusion(f32[2048,512]{1,0:T(8,128)} %fusion.5, bf16[2048,768]{1,0:T(8,128)(2,1)} %all-gather.3.cloned.1.call-done, bf16[64,768]{1,0:T(8,128)(2,1)S(1)} %reshape.38, bf16[64,8192]{1,0:T(8,128)(2,1)S(1)} %slice.18, s32[]{:T(128)S(6)} %select_n.3), kind=kOutput, calls=%fused_computation.1 | convolution fusion | flops 338821120 | bytes 9601028 | tf_op jit(solution)/shard_map/dot_general | solution.py:45
  110.3 3.1 %copy.16 = bf16[4,4,128,512]{3,2,0,1:T(8,128)(2,1)} copy(bf16[4,4,128,512]{3,2,1,0:T(8,128)(2,1)} %bitcast.21) | data formatting | bytes 4194304 | tf_op jit(solution)/shard_map/reshape | solution.py:51
  113.4 4.5 %all-to-all-start = ((bf16[4,512,512]{2,1,0:T(8,128)(2,1)}), bf16[4,512,512]{2,1,0:T(8,128)(2,1)}, u32[]{:S(2)}, u32[]{:S(2)}) async-start(bf16[4,512,512]{2,1,0:T(8,128)(2,1)} %bitcast.23), calls=%async_computation | async-start | bytes 4194304 | tf_op jit(solution)/shard_map/all_to_all | solution.py:56
  117.9 3.1 %pad_maximum_fusion = f32[573440]{0:T(1024)} fusion(f32[49152]{0:T(1024)S(1)} %reshape.41, f32[524288]{0:T(1024)} %bitcast.22), kind=kLoop, calls=%fused_computation.3 | loop fusion | flops 573440 | bytes 4587520 | tf_op jit(solution)/shard_map/concatenate | solution.py:29
  121.0 60.2 %all-to-all-done = bf16[4,512,512]{2,1,0:T(8,128)(2,1)} async-done(((bf16[4,512,512]{2,1,0:T(8,128)(2,1)}), bf16[4,512,512]{2,1,0:T(8,128)(2,1)}, u32[]{:S(2)}, u32[]{:S(2)}) %all-to-all-start) | async-done | bytes 2097184 | tf_op jit(solution)/shard_map/all_to_all | solution.py:56
  181.3 4.5 %copy.17 = bf16[512,4,512]{2,1,0:T(4,128)(2,1)} copy(bf16[512,4,512]{2,0,1:T(8,128)(2,1)} %bitcast.3) | data formatting | bytes 4194304 | tf_op jit(solution)/shard_map/all_to_all | solution.py:56
  185.8 4.5 %all_to_all.29 = bf16[4,128,2048]{2,1,0:T(8,128)(2,1)} reshape(bf16[512,4,512]{2,1,0:T(4,128)(2,1)} %copy.17) | data formatting | bytes 4194304 | tf_op jit(solution)/shard_map/all_to_all | solution.py:55
  190.3 4.6 %all-to-all-start.1 = ((bf16[4,128,2048]{2,1,0:T(8,128)(2,1)}), bf16[4,128,2048]{2,1,0:T(8,128)(2,1)}, u32[]{:S(2)}, u32[]{:S(2)}) async-start(bf16[4,128,2048]{2,1,0:T(8,128)(2,1)} %all_to_all.29), calls=%async_computation.1 | async-start | bytes 4194304 | tf_op jit(solution)/shard_map/all_to_all | solution.py:55
  196.2 53.3 %all-reduce.3.cloned.1.call-done = f32[573440]{0:T(1024)} async-done(((f32[573440]{0:T(1024)}), f32[573440]{0:T(1024)}) %all-reduce.3.cloned.1.call-update) | async-done | bytes 2293776
  249.5 1.5 multiply_reduce_fusion
  251.0 31.8 %psum.7 = f32[]{:T(128)} all-reduce(f32[]{:T(128)} %multiply_reduce_fusion), channel_id=1, replica_groups=mesh['groups'=2,'outer'=4,'inner'=4] {'outer','inner'}, use_global_device_ids=true, to_apply=%region_2.0 | all-reduce | flops 1 | bytes 8 | tf_op jit(solution)/shard_map/psum | solution.py:31
  283.5 1.7 divide_subtract_fusion
  285.2 3.9 %copy.18 = bf16[128,4,2048]{0,2,1:T(8,128)(2,1)} copy(bf16[128,4,2048]{2,0,1:T(8,128)(2,1)} %bitcast.4) | data formatting | bytes 4194304 | tf_op jit(solution)/shard_map/all_to_all | solution.py:55
  289.2 4.1 %copy.19 = bf16[128,8192]{1,0:T(8,128)(2,1)} copy(bf16[128,8192]{0,1:T(8,128)(2,1)} %bitcast.24) | data formatting | bytes 4194304
  (23 shorter events, 1.6 us)
Async XLA Ops:
  7.2 48.6 %copy-start = (bf16[128,8192]{1,0:T(8,128)(2,1)S(1)}, bf16[128,8192]{1,0:T(8,128)(2,1)}, u32[]{:S(2)}) copy-start(bf16[128,8192]{1,0:T(8,128)(2,1)} %param.6) | copy-start | bytes 6291460
  7.2 44.6 %all-gather.5.cloned.1.call-start = ((), (), s32[]{:S(2)}) async-start(), calls=%async_computation.3 | async-start | bytes 1218560 | tf_op jit(solution)/shard_map/all_gather | solution.py:12
  8.9 89.4 %all-gather.3.cloned.1.call-start = ((), (), s32[]{:S(2)}) async-start(), calls=%async_computation.2 | async-start | bytes 3342336 | tf_op jit(solution)/shard_map/all_gather | solution.py:35
  9.7 46.1 %copy-start.1 = (bf16[128,768]{1,0:T(8,128)(2,1)S(1)}, bf16[128,768]{1,0:T(8,128)(2,1)}, u32[]{:S(2)}) copy-start(bf16[128,768]{1,0:T(8,128)(2,1)} %param.7) | copy-start | bytes 589828
  51.8 3.8 %slice-start = ((bf16[573440]{0:T(1024)(128)(2,1)}), bf16[49152]{0:T(1024)(128)(2,1)S(1)}, s32[]{:S(2)}) async-start(bf16[573440]{0:T(1024)(128)(2,1)} %all-gather.5.cloned.1.call-done), calls=%async_computation.5 | async-start | bytes 196608 | tf_op jit(solution)/shard_map/slice | solution.py:16
  113.4 67.9 %all-to-all-start = ((bf16[4,512,512]{2,1,0:T(8,128)(2,1)}), bf16[4,512,512]{2,1,0:T(8,128)(2,1)}, u32[]{:S(2)}, u32[]{:S(2)}) async-start(bf16[4,512,512]{2,1,0:T(8,128)(2,1)} %bitcast.23), calls=%async_computation | async-start | bytes 4194304 | tf_op jit(solution)/shard_map/all_to_all | solution.py:56
  117.8 131.7 %all-reduce.3.cloned.1.call-start = ((), (), s32[]{:S(2)}) async-start(), calls=%async_computation.4 | async-start | bytes 4587520
  190.3 4.6 %copy-start.5 = (u32[32]{0:T(128)S(1)}, u32[32]{0:T(128)}, u32[]{:S(2)}) copy-start(u32[32]{0:T(128)} %constant.46) | copy-start | bytes 388
  190.3 93.2 %copy-start.2 = (f32[35840]{0:T(1024)S(1)}, f32[35840]{0:T(1024)}, u32[]{:S(2)}) copy-start(f32[35840]{0:T(1024)} %param.9) | copy-start | bytes 430084
  190.3 93.2 %copy-start.3 = (f32[35840]{0:T(1024)S(1)}, f32[35840]{0:T(1024)}, u32[]{:S(2)}) copy-start(f32[35840]{0:T(1024)} %param.10) | copy-start | bytes 430084
  190.3 93.2 %copy-start.4 = (f32[35840]{0:T(1024)S(1)}, f32[35840]{0:T(1024)}, u32[]{:S(2)}) copy-start(f32[35840]{0:T(1024)} %param.11) | copy-start | bytes 430084
  190.3 94.9 %all-to-all-start.1 = ((bf16[4,128,2048]{2,1,0:T(8,128)(2,1)}), bf16[4,128,2048]{2,1,0:T(8,128)(2,1)}, u32[]{:S(2)}, u32[]{:S(2)}) async-start(bf16[4,128,2048]{2,1,0:T(8,128)(2,1)} %all_to_all.29), calls=%async_computation.1 | async-start | bytes 4194304 | tf_op jit(solution)/shard_map/all_to_all | solution.py:55
Sparse Core Ops, SparseCore 0:
  10.8 40.9 all-gather.4
  54.1 44.1 all-gather.2
  122.2 127.1 all-reduce.2
where the time goes:
time: 301 us; the launch traced here: 300 us
  waiting for transfers between devices  191 us (63%)
  blocking collectives  31.8 us (11%)
  local copies, waits for them, and re-layouts  29 us (10%)
  matrix products  15.7 us (5%)
  between operations  15.2 us (5%)
  starting transfers between devices  9.18 us (3%)
  other arithmetic  8.1 us (3%)
    all_to_all x1, waiting for transfers between devices, per_device(): lax.all_to_all(reordered, 'inner', split_axis=0, concat_axis=1, tiled=True)  60.2 us
    unnamed x4, waiting for transfers between devices  54 us
    all_gather x1, waiting for transfers between devices, per_device(): lax.all_gather(master.astype(jnp.bfloat16), ('outer', 'inner'), axis=0, t...  42.1 us
    all_gather x1, waiting for transfers between devices, per_device(): tok_piece = lax.all_gather(upstream, ('outer', 'inner'), axis=0, tiled=True)  34.5 us
    psum x1, blocking collectives, per_device(): sum_squares = lax.psum(jnp.sum(grad_shard * grad_shard), ('outer', 'inner'))  31.8 us
    all_to_all x2, local copies, waits for them, and re-layouts, per_device(): lax.all_to_all(lax.all_to_all(reordered, 'inner', split_axis=0, concat_ax...  8.44 us
    unnamed x15, local copies, waits for them, and re-layouts  8.05 us
    dot_general x1, matrix products, per_device(): jnp.dot(rank_piece, own_cols, preferred_element_type=jnp.float32)  6.09 us
  transfers between devices with their start and end apart: 5, of which 4 were waited for; matrix products, arithmetic and copies ran while one was open for 8% of the time, Pallas kernels for 0%

commit v1 on v0

--- a/solution.py
+++ b/solution.py
@@ -1,9 +1,16 @@
+import functools
 import math
 
 import jax
 import jax.numpy as jnp
 from jax import lax
+from jax.experimental import pallas as pl
+from jax.experimental.pallas import tpu as pltpu
 from jax.sharding import PartitionSpec as P
+
+MESH = pl.DeviceIdType.MESH
+LANES = 128
+CHUNK = 1024
 
 
 def per_device(activations, upstream, frozen_weight_matrix, master, moment, second_moment):
@@ -59,19 +66,323 @@
         concat_axis=1,
         tiled=True,
     )
+    new_master, new_moment, new_second = adam(
+        grad_shard, sum_squares, master, moment, second_moment, whole.shape[0]
+    )
+    return (input_gradient_rows, new_master, new_moment, new_second)
+
+
+def adam(grad_shard, sum_squares, master, moment, second_moment, params):
     norm = jnp.sqrt(sum_squares + 1e-06)
-    clipped = grad_shard * jnp.minimum(1.0, math.sqrt(whole.shape[0]) / norm)
+    clipped = grad_shard * jnp.minimum(1.0, math.sqrt(params) / norm)
     new_moment = 0.9 * moment + 0.1 * clipped
     new_second = 0.999 * second_moment + 0.001 * clipped * clipped
     corr_one = 1.0 - 0.9**10
     corr_two = 1.0 - 0.999**10
     new_master = master - 0.1 * (new_moment / corr_one) / (jnp.sqrt(new_second / corr_two) + 1e-08)
-    return (input_gradient_rows, new_master, new_moment, new_second)
+    return new_master, new_moment, new_second
+
+
+def dot(a, b, contract):
+    return lax.dot_general(
+        a, b, (((contract[0],), (contract[1],)), ((), ())), preferred_element_type=jnp.float32
+    )
+
+
+def kernel(
+    rank,
+    act_ref,
+    up_ref,
+    w_ref,
+    master_ref,
+    moment_ref,
+    second_ref,
+    out_ref,
+    new_master_ref,
+    new_moment_ref,
+    new_second_ref,
+    slots,
+    flat,
+    down,
+    up_all,
+    w_buf,
+    grad,
+    from_core,
+    half_sum,
+    from_x,
+    from_z,
+    sq_own,
+    sq_z,
+    sq_line,
+    sq_s,
+    blocks,
+    send_sem,
+    recv_sem,
+):
+    y = lax.axis_index("groups")
+    o = lax.axis_index("outer")
+    z = lax.axis_index("inner")
+    x, c = o // 2, lax.rem(o, 2)
+    o_core = 2 * x + (1 - c)
+    o_x = 2 * (1 - x) + c
+    o_diag = 2 * (1 - x) + (1 - c)
+    core_dev, x_dev, diag_dev = {"outer": o_core}, {"outer": o_x}, {"outer": o_diag}
+    y_dev = {"groups": 1 - y}
+    z_to = [None] + [lax.rem(z + k, 4) for k in range(1, 4)]
+    z_from = [z] + [lax.rem(z + 4 - k, 4) for k in range(1, 4)]
+    z_devs = [None] + [{"inner": z_to[k]} for k in range(1, 4)]
+
+    tokens, width = act_ref.shape
+    value_width = up_ref.shape[1]
+    feats = w_ref.shape[0]
+    half = feats // 2
+    shard_rows = master_ref.shape[0]
+    down_rows = rank * width // LANES
+    params = 16 * shard_rows * LANES
+    scale = 0.5 / math.sqrt(rank * value_width)
+
+    used = []
+
+    def send(src, dst, device):
+        at = len(used)
+        copy = pltpu.make_async_remote_copy(
+            src_ref=src,
+            dst_ref=dst,
+            send_sem=send_sem.at[at],
+            recv_sem=recv_sem.at[at],
+            device_id=device,
+            device_id_type=MESH,
+        )
+        used.append(copy)
+        copy.start()
+        return copy
+
+    own = o * 4 + z
+    pad = slots.shape[1] - shard_rows
+    slots[own] = jnp.concatenate(
+        [master_ref[...], jnp.zeros((pad, LANES), jnp.float32)], axis=0
+    ).astype(jnp.bfloat16)
+    up_all[o] = up_ref[...]
+
+    barrier = pltpu.get_barrier_semaphore()
+    partners = [core_dev, x_dev, diag_dev, y_dev] + z_devs[1:]
+    for device in partners:
+        pl.semaphore_signal(barrier, inc=1, device_id=device, device_id_type=MESH)
+    pl.semaphore_wait(barrier, len(partners))
+
+    slot_z = [None] + [send(slots.at[own], slots.at[own], z_devs[k]) for k in range(1, 4)]
+    slot_x = [send(slots.at[own], slots.at[own], x_dev)]
+    slot_core = [send(slots.at[own], slots.at[own], core_dev)]
+    u_x = send(up_all.at[o], up_all.at[o], x_dev)
+    u_core = send(up_all.at[o], up_all.at[o], core_dev)
+    my_half = pl.ds(pl.multiple_of(y * half, half), half)
+    w_z = [None] + [
+        send(w_ref.at[my_half], w_buf.at[k - 1, my_half], z_devs[k]) for k in range(1, 4)
+    ]
+    for k in range(1, 4):
+        slot_z[k].wait_recv()
+        at = slots.at[o * 4 + z_from[k]]
+        slot_x.append(send(at, at, x_dev))
+        slot_core.append(send(at, at, core_dev))
+    for k in range(4):
+        slot_x[k].wait_recv()
+        at = slots.at[o_x * 4 + z_from[k]]
+        slot_core.append(send(at, at, core_dev))
+    u_x.wait_recv()
+    u_far = send(up_all.at[o_x], up_all.at[o_x], core_dev)
+    w_y = [None]
+
+    def pass_weight(k):
+        w_z[k].wait_recv()
+        at = w_buf.at[k - 1, my_half]
+        w_y.append(send(at, at, y_dev))
+
+    for copy in slot_core:
+        copy.wait_recv()
+    for d in range(16):
+        flat[d * shard_rows : (d + 1) * shard_rows, :] = slots[d].astype(jnp.float32)[:shard_rows]
+
+    per_up = value_width // LANES
+    up_m = jnp.concatenate(
+        [flat[pl.ds(down_rows + j, rank, stride=per_up), :] for j in range(per_up)], axis=1
+    ).astype(jnp.bfloat16)
+    own_rank = dot(up_ref[...], up_m, (1, 1)).astype(jnp.bfloat16)
+    per_row = width // LANES
+
+    def part(n, projected):
+        cols = pl.ds(pl.multiple_of(n * CHUNK, CHUNK), CHUNK)
+        rows = [pl.ds(n * (CHUNK // LANES) + j, rank, stride=per_row) for j in range(CHUNK // LANES)]
+        d_part = jnp.concatenate([flat[r, :] for r in rows], axis=1).astype(jnp.bfloat16)
+        down[:, cols] = d_part
+        a_part = act_ref[:, cols]
+        g_part = scale * dot(own_rank, a_part, (0, 0))
+        for j, r in enumerate(rows):
+            grad[r, :] = g_part[:, j * LANES : (j + 1) * LANES]
+        return projected + dot(a_part, d_part, (1, 1))
+
+    projected = lax.fori_loop(
+        0, width // CHUNK, part, jnp.zeros((tokens, rank), jnp.float32)
+    ).astype(jnp.bfloat16)
+    g_up = scale * dot(projected, up_ref[...], (0, 0))
+    for j in range(per_up):
+        grad[pl.ds(down_rows + j, rank, stride=per_up), :] = g_up[:, j * LANES : (j + 1) * LANES]
+
+    quarter = 4 * shard_rows
+
+    def grad_rows(at):
+        return pl.ds(pl.multiple_of(at * quarter, quarter), quarter)
+
+    g_core_far = send(grad.at[grad_rows(o_diag)], from_core.at[0], core_dev)
+    g_core_own = send(grad.at[grad_rows(o_core)], from_core.at[1], core_dev)
+    pass_weight(1)
+    u_core.wait_recv()
+    u_far.wait_recv()
+    u_rows = 4 * tokens
+    rank_all = dot(up_all[...].reshape(u_rows, value_width), up_m, (1, 1)).astype(jnp.bfloat16)
+
+    block_copies = []
+
+    def block_math(k):
+        first = pl.multiple_of((o * 4 + z_from[k]) * feats, feats)
+        w = w_ref[...] if k == 0 else w_buf[k - 1]
+        value = dot(up_all[...].reshape(u_rows, value_width), w, (1, 1)) + scale * dot(
+            rank_all, down[:, pl.ds(first, feats)], (1, 0)
+        )
+        blocks[k] = value.astype(jnp.bfloat16).reshape(4, tokens, feats)
+        out_ref[:, pl.ds(first, feats)] = blocks[k, o]
+
+    def block_send(k):
+        first = pl.multiple_of((o * 4 + z_from[k]) * feats, feats)
+        for to, device in ((o_x, x_dev), (o_diag, diag_dev), (o_core, core_dev)):
+            block_copies.append(
+                send(blocks.at[k, to], out_ref.at[:, pl.ds(first, feats)], device)
+            )
+
+    block_math(0)
+    g_core_far.wait_recv()
+    half_sum[0] = grad[grad_rows(o_x), :] + from_core[0]
+    g_x = send(half_sum.at[0], from_x, x_dev)
+    block_send(0)
+    g_core_own.wait_recv()
+    half_sum[1] = grad[grad_rows(o), :] + from_core[1]
+    pass_weight(2)
+    w_y[1].wait_recv()
+    block_math(1)
+    block_send(1)
+    g_x.wait_recv()
+    half_sum[1] += from_x[...]
+
+    def shard(at):
+        return pl.ds(pl.multiple_of(at * shard_rows, shard_rows), shard_rows)
+
+    g_z = [
+        send(half_sum.at[1, shard(z_to[k])], from_z.at[k - 1], z_devs[k]) for k in range(1, 4)
+    ]
+    pass_weight(3)
+    w_y[2].wait_recv()
+    block_math(2)
+    block_send(2)
+    for copy in g_z:
+        copy.wait_recv()
+    total = half_sum[1, shard(z), :] + from_z[0] + from_z[1] + from_z[2]
+    grad_total = total
+    sq_own[...] = jnp.sum((total * total).reshape(shard_rows // 8, 8, LANES), axis=0)
+    s_z = [send(sq_own, sq_z.at[k - 1], z_devs[k]) for k in range(1, 4)]
+    w_y[3].wait_recv()
+    block_math(3)
+    block_send(3)
+    for copy in s_z:
+        copy.wait_recv()
+    sq_line[...] = sq_own[...] + sq_z[0] + sq_z[1] + sq_z[2]
+    s_s = [
+        send(sq_line, sq_s.at[n], device)
+        for n, device in enumerate((core_dev, x_dev, diag_dev))
+    ]
+    for copy in s_s:
+        copy.wait_recv()
+    sum_squares = jnp.sum(sq_line[...] + sq_s[0] + sq_s[1] + sq_s[2], keepdims=True)
+    new_master_ref[...], new_moment_ref[...], new_second_ref[...] = adam(
+        grad_total, sum_squares, master_ref[...], moment_ref[...], second_ref[...], params
+    )
+    for copy in block_copies:
+        copy.wait_recv()
+    for copy in used:
+        copy.wait_send()
+
+
+N_COPIES = 64
+
+
+def fused(rank, activations, upstream, weight, master, moment, second_moment):
+    tokens, width = activations.shape
+    value_width = upstream.shape[1]
+    feats = weight.shape[0]
+    shard_rows = master.shape[0] // LANES
+    flat_rows = 16 * shard_rows
+    padded = -(-shard_rows // 16) * 16
+    state = jax.ShapeDtypeStruct((shard_rows, LANES), jnp.float32)
+    bf16, f32 = jnp.bfloat16, jnp.float32
+    vmem = pl.BlockSpec(memory_space=pltpu.VMEM)
+    result = pl.pallas_call(
+        functools.partial(kernel, rank),
+        out_shape=(jax.ShapeDtypeStruct((tokens, width), bf16), state, state, state),
+        in_specs=[vmem] * 6,
+        out_specs=(vmem,) * 4,
+        scratch_shapes=[
+            pltpu.VMEM((16, padded, LANES), bf16),
+            pltpu.VMEM((flat_rows, LANES), f32),
+            pltpu.VMEM((rank, width), bf16),
+            pltpu.VMEM((4, tokens, value_width), bf16),
+            pltpu.VMEM((3, feats, value_width), bf16),
+            pltpu.VMEM((flat_rows, LANES), f32),
+            pltpu.VMEM((2, 4 * shard_rows, LANES), f32),
+            pltpu.VMEM((2, 4 * shard_rows, LANES), f32),
+            pltpu.VMEM((4 * shard_rows, LANES), f32),
+            pltpu.VMEM((3, shard_rows, LANES), f32),
+            pltpu.VMEM((8, LANES), f32),
+            pltpu.VMEM((3, 8, LANES), f32),
+            pltpu.VMEM((8, LANES), f32),
+            pltpu.VMEM((3, 8, LANES), f32),
+            pltpu.VMEM((4, 4, tokens, feats), bf16),
+            pltpu.SemaphoreType.DMA((N_COPIES,)),
+            pltpu.SemaphoreType.DMA((N_COPIES,)),
+        ],
+        compiler_params=pltpu.CompilerParams(
+            collective_id=0, has_side_effects=True, vmem_limit_bytes=52 * 1024 * 1024
+        ),
+        name="adapter_backward",
+    )(
+        activations,
+        upstream,
+        weight,
+        master.reshape(shard_rows, LANES),
+        moment.reshape(shard_rows, LANES),
+        second_moment.reshape(shard_rows, LANES),
+    )
+    return (result[0],) + tuple(r.reshape(-1) for r in result[1:])
 
 
 def solution(mesh):
+    sizes = dict(mesh.shape)
+    square = sizes["groups"] == 2 and sizes["outer"] == 4 and sizes["inner"] == 4
+
+    def body(activations, upstream, weight, master, moment, second_moment):
+        width, value_width = activations.shape[1], upstream.shape[1]
+        rank = master.shape[0] * sizes["outer"] * sizes["inner"] // (width + value_width)
+        fits = (
+            activations.shape[0] % 16 == 0
+            and width % CHUNK == 0
+            and value_width % LANES == 0
+            and weight.shape[0] % 256 == 0
+            and master.shape[0] % (8 * LANES) == 0
+            and rank % 16 == 0
+        )
+        if square and fits:
+            return fused(rank, activations, upstream, weight, master, moment, second_moment)
+        return per_device(activations, upstream, weight, master, moment, second_moment)
+
     return jax.shard_map(
-        per_device,
+        body,
         mesh=mesh,
         in_specs=(
             P(("groups", "outer", "inner"), None),

time: 301 us -> 89.9 us (0.30)
  waiting for transfers between devices: 191 us -> 0 us
  Pallas kernels: 0 us -> 78.8 us
  blocking collectives: 31.8 us -> 0 us
  local copies, waits for them, and re-layouts: 29 us -> 9.88 us
  matrix products: 15.7 us -> 0 us
  between operations: 15.2 us -> 0.65 us
  starting transfers between devices: 9.18 us -> 0 us
  other arithmetic: 8.1 us -> 0 us
    pallas_call x0 -> x1, Pallas kernels: none -> 78.8 us  [fused(): pl.pallas_call(functools.partial(kernel, rank), out_shape=(jax.ShapeDtype...]
    all_gather x2 -> x0, waiting for transfers between devices: 76.6 us -> none  [the longest x1 42.1 us: per_device(): lax.all_gather(master.astype(jnp.bfloat16), ('outer', 'inner'), axis=0, t...]
    all_to_all x2 -> x0, waiting for transfers between devices: 60.3 us -> none  [the longest x1 60.2 us: per_device(): lax.all_to_all(reordered, 'inner', split_axis=0, concat_axis=1, tiled=True)]
    unnamed x4 -> x0, waiting for transfers between devices: 54 us -> none
    psum x1 -> x0, blocking collectives: 31.8 us -> none  [per_device(): sum_squares = lax.psum(jnp.sum(grad_shard * grad_shard), ('outer', 'inner'))]
    dot_general x4 -> x0, matrix products: 15.7 us -> none  [the longest x1 6.09 us: per_device(): jnp.dot(rank_piece, own_cols, preferred_element_type=jnp.float32)]
    all_to_all x3 -> x0, local copies, waits for them, and re-layouts: 13 us -> none  [the longest x2 8.44 us: per_device(): lax.all_to_all(lax.all_to_all(reordered, 'inner', split_axis=0, concat_ax...]
    all_to_all x2 -> x0, starting transfers between devices: 9.06 us -> none  [the longest x1 4.6 us: per_device(): lax.all_to_all(lax.all_to_all(reordered, 'inner', split_axis=0, concat_ax...]
  transfers between devices with their start and end apart: 5 -> 0, of which waited for: 4 -> 0; matrix products, arithmetic and copies ran while one was open for 8% -> 0% of each run, Pallas kernels for 0% -> 0%
where the time goes in v1:
time: 89.9 us; the launch traced here: 89.3 us
  Pallas kernels  78.8 us (88%)
  local copies, waits for them, and re-layouts  9.88 us (11%)
    pallas_call x1, Pallas kernels, fused(): pl.pallas_call(functools.partial(kernel, rank), out_shape=(jax.ShapeDtype...  78.8 us
    unnamed x14, local copies, waits for them, and re-layouts  9.88 us

profile of v1, /device:TPU:0, one launch (start us, length us, event | category | flops | bytes accessed | tf_op | source)
XLA Modules:
  0.0 89.3 jit_solution(10584817222058289105)
XLA Ops:
  0.6 0.0 copy-start
  0.6 1.1 %copy-done = bf16[512,768]{1,0:T(8,128)(2,1)S(1)} copy-done((bf16[512,768]{1,0:T(8,128)(2,1)S(1)}, bf16[512,768]{1,0:T(8,128)(2,1)}, u32[]{:S(2)}) %copy-start) | copy-done | bytes 786456
  1.8 0.0 copy-start.1
  1.8 0.9 %copy-done.1 = bf16[128,768]{1,0:T(8,128)(2,1)S(1)} copy-done((bf16[128,768]{1,0:T(8,128)(2,1)S(1)}, bf16[128,768]{1,0:T(8,128)(2,1)}, u32[]{:S(2)}) %copy-start.1) | copy-done | bytes 196632
  2.7 0.0 copy-start.2
  2.7 0.9 %copy-done.2 = f32[35840]{0:T(1024)S(1)} copy-done((f32[35840]{0:T(1024)S(1)}, f32[35840]{0:T(1024)}, u32[]{:S(2)}) %copy-start.2) | copy-done | bytes 143384
  3.6 0.0 copy-start.3
  3.6 0.9 %copy-done.3 = f32[35840]{0:T(1024)S(1)} copy-done((f32[35840]{0:T(1024)S(1)}, f32[35840]{0:T(1024)}, u32[]{:S(2)}) %copy-start.3) | copy-done | bytes 143384
  4.5 0.0 copy-start.4
  4.5 0.9 %copy-done.4 = f32[35840]{0:T(1024)S(1)} copy-done((f32[35840]{0:T(1024)S(1)}, f32[35840]{0:T(1024)}, u32[]{:S(2)}) %copy-start.4) | copy-done | bytes 143384
  5.4 78.8 %adapter_backward.1 = (bf16[128,8192]{1,0:T(8,128)(2,1)}, f32[280,128]{1,0:T(8,128)S(1)}, f32[280,128]{1,0:T(8,128)S(1)}, f32[280,128]{1,0:T(8,128)S(1)}) custom-call(bf16[128,8192]{1,0:T(8,128)(2,1)} %act_ref.1, bf16[128,768]{1,0:T(8,128)(2,1)S(1)} %copy-done.1, bf16[512,768]{1,0:T(8,128)(2,1)S(1)} %copy-done, f32[280,128]{1,0:T(8,128)S(1)} %bitcast.9, ...), custom_call_target="tpu_custom_call" | custom-call | tf_op jit(solution)/shard_map/adapter_backward/pallas_call | solution.py:326
  84.2 3.1 %copy.14 = bf16[128,8192]{1,0:T(8,128)(2,1)} copy(bf16[128,8192]{1,0:T(8,128)(2,1)} %get-tuple-element.16) | data formatting | bytes 4194304
  87.3 0.7 copy.15
  88.0 0.7 copy.16
  88.7 0.7 copy.17
Async XLA Ops:
  0.6 1.1 %copy-start = (bf16[512,768]{1,0:T(8,128)(2,1)S(1)}, bf16[512,768]{1,0:T(8,128)(2,1)}, u32[]{:S(2)}) copy-start(bf16[512,768]{1,0:T(8,128)(2,1)} %w_ref.1) | copy-start | bytes 2359300
  1.8 0.9 %copy-start.1 = (bf16[128,768]{1,0:T(8,128)(2,1)S(1)}, bf16[128,768]{1,0:T(8,128)(2,1)}, u32[]{:S(2)}) copy-start(bf16[128,768]{1,0:T(8,128)(2,1)} %up_ref.1) | copy-start | bytes 589828
  2.7 0.9 %copy-start.2 = (f32[35840]{0:T(1024)S(1)}, f32[35840]{0:T(1024)}, u32[]{:S(2)}) copy-start(f32[35840]{0:T(1024)} %param.9) | copy-start | bytes 430084
  3.6 0.9 %copy-start.3 = (f32[35840]{0:T(1024)S(1)}, f32[35840]{0:T(1024)}, u32[]{:S(2)}) copy-start(f32[35840]{0:T(1024)} %param.10) | copy-start | bytes 430084
  4.5 0.9 %copy-start.4 = (f32[35840]{0:T(1024)S(1)}, f32[35840]{0:T(1024)}, u32[]{:S(2)}) copy-start(f32[35840]{0:T(1024)} %param.11) | copy-start | bytes 430084

commit v2 on v1

--- a/solution.py
+++ b/solution.py
@@ -66,15 +66,12 @@
         concat_axis=1,
         tiled=True,
     )
-    new_master, new_moment, new_second = adam(
-        grad_shard, sum_squares, master, moment, second_moment, whole.shape[0]
-    )
-    return (input_gradient_rows, new_master, new_moment, new_second)
-
-
-def adam(grad_shard, sum_squares, master, moment, second_moment, params):
     norm = jnp.sqrt(sum_squares + 1e-06)
-    clipped = grad_shard * jnp.minimum(1.0, math.sqrt(params) / norm)
+    clipped = grad_shard * jnp.minimum(1.0, math.sqrt(whole.shape[0]) / norm)
+    return (input_gradient_rows,) + adam(clipped, master, moment, second_moment)
+
+
+def adam(clipped, master, moment, second_moment):
     new_moment = 0.9 * moment + 0.1 * clipped
     new_second = 0.999 * second_moment + 0.001 * clipped * clipped
     corr_one = 1.0 - 0.9**10
@@ -91,16 +88,14 @@
 
 def kernel(
     rank,
+    act_hbm,
+    up_hbm,
+    w_hbm,
+    master_hbm,
+    out_ref,
+    clipped_ref,
     act_ref,
-    up_ref,
-    w_ref,
     master_ref,
-    moment_ref,
-    second_ref,
-    out_ref,
-    new_master_ref,
-    new_moment_ref,
-    new_second_ref,
     slots,
     flat,
     down,
@@ -116,8 +111,11 @@
     sq_line,
     sq_s,
     blocks,
+    load_sem,
     send_sem,
     recv_sem,
+    w_send_sem,
+    w_recv_sem,
 ):
     y = lax.axis_index("groups")
     o = lax.axis_index("outer")
@@ -131,15 +129,38 @@
     z_to = [None] + [lax.rem(z + k, 4) for k in range(1, 4)]
     z_from = [z] + [lax.rem(z + 4 - k, 4) for k in range(1, 4)]
     z_devs = [None] + [{"inner": z_to[k]} for k in range(1, 4)]
+    high = z // 2
+    u = z + high * (3 - 2 * z)
+    order = [z] + [f + high * (3 - 2 * f) for f in (1 - u, 2, 3)]
 
     tokens, width = act_ref.shape
-    value_width = up_ref.shape[1]
-    feats = w_ref.shape[0]
+    value_width = up_all.shape[2]
+    feats = w_buf.shape[1]
     half = feats // 2
     shard_rows = master_ref.shape[0]
     down_rows = rank * width // LANES
     params = 16 * shard_rows * LANES
     scale = 0.5 / math.sqrt(rank * value_width)
+
+    barrier = pltpu.get_barrier_semaphore()
+    partners = [core_dev, x_dev, diag_dev, y_dev] + z_devs[1:]
+    for device in partners:
+        pl.semaphore_signal(barrier, inc=1, device_id=device, device_id_type=MESH)
+
+    loads = [
+        pltpu.make_async_copy(src, dst, load_sem.at[n])
+        for n, (src, dst) in enumerate(
+            (
+                (master_hbm, master_ref),
+                (up_hbm, up_all.at[o]),
+                (w_hbm, w_buf.at[z]),
+                (act_hbm, act_ref),
+            )
+        )
+    ]
+    for load in loads:
+        load.start()
+    load_master, load_up, load_w, load_act = loads
 
     used = []
 
@@ -159,26 +180,63 @@
 
     own = o * 4 + z
     pad = slots.shape[1] - shard_rows
+    load_master.wait()
     slots[own] = jnp.concatenate(
         [master_ref[...], jnp.zeros((pad, LANES), jnp.float32)], axis=0
     ).astype(jnp.bfloat16)
-    up_all[o] = up_ref[...]
-
-    barrier = pltpu.get_barrier_semaphore()
-    partners = [core_dev, x_dev, diag_dev, y_dev] + z_devs[1:]
-    for device in partners:
-        pl.semaphore_signal(barrier, inc=1, device_id=device, device_id_type=MESH)
     pl.semaphore_wait(barrier, len(partners))
+
+    my_half = pl.ds(pl.multiple_of(y * half, half), half)
+    other_half = pl.ds(pl.multiple_of((1 - y) * half, half), half)
+
+    def weight_copy(b, way, device):
+        at = w_buf.at[b, my_half]
+        return pltpu.make_async_remote_copy(
+            src_ref=at,
+            dst_ref=at,
+            send_sem=w_send_sem.at[way, b],
+            recv_sem=w_recv_sem.at[way // 2, b],
+            device_id=device,
+            device_id_type=MESH,
+        )
+
+    def weight_up(b):
+        return weight_copy(b, 0, {"inner": z + 1})
+
+    def weight_down(b):
+        return weight_copy(b, 1, {"inner": z - 1})
+
+    def weight_y(b):
+        return weight_copy(b, 2, y_dev)
+
+    goes_up = lambda b: (b <= z) & (z < 3)
+    goes_down = lambda b: (b >= z) & (z > 0)
+
+    def pass_on(b):
+        pl.when(goes_up(b))(lambda: weight_up(b).start())
+        pl.when(goes_down(b))(lambda: weight_down(b).start())
+
+    def arrive(n):
+        b = order[n]
+        pltpu.make_async_remote_copy(
+            src_ref=w_buf.at[b, my_half],
+            dst_ref=w_buf.at[b, my_half],
+            send_sem=w_send_sem.at[0, b],
+            recv_sem=w_recv_sem.at[0, b],
+            device_id=y_dev,
+            device_id_type=MESH,
+        ).wait_recv()
+        pass_on(b)
+        weight_y(b).start()
 
     slot_z = [None] + [send(slots.at[own], slots.at[own], z_devs[k]) for k in range(1, 4)]
     slot_x = [send(slots.at[own], slots.at[own], x_dev)]
     slot_core = [send(slots.at[own], slots.at[own], core_dev)]
+    load_w.wait()
+    pass_on(z)
+    load_up.wait()
     u_x = send(up_all.at[o], up_all.at[o], x_dev)
     u_core = send(up_all.at[o], up_all.at[o], core_dev)
-    my_half = pl.ds(pl.multiple_of(y * half, half), half)
-    w_z = [None] + [
-        send(w_ref.at[my_half], w_buf.at[k - 1, my_half], z_devs[k]) for k in range(1, 4)
-    ]
     for k in range(1, 4):
         slot_z[k].wait_recv()
         at = slots.at[o * 4 + z_from[k]]
@@ -190,12 +248,9 @@
         slot_core.append(send(at, at, core_dev))
     u_x.wait_recv()
     u_far = send(up_all.at[o_x], up_all.at[o_x], core_dev)
-    w_y = [None]
-
-    def pass_weight(k):
-        w_z[k].wait_recv()
-        at = w_buf.at[k - 1, my_half]
-        w_y.append(send(at, at, y_dev))
+    middle = u == 1
+    arrive(1)
+    pl.when(middle)(lambda: arrive(2))
 
     for copy in slot_core:
         copy.wait_recv()
@@ -206,8 +261,9 @@
     up_m = jnp.concatenate(
         [flat[pl.ds(down_rows + j, rank, stride=per_up), :] for j in range(per_up)], axis=1
     ).astype(jnp.bfloat16)
-    own_rank = dot(up_ref[...], up_m, (1, 1)).astype(jnp.bfloat16)
+    own_rank = dot(up_all[o], up_m, (1, 1)).astype(jnp.bfloat16)
     per_row = width // LANES
+    load_act.wait()
 
     def part(n, projected):
         cols = pl.ds(pl.multiple_of(n * CHUNK, CHUNK), CHUNK)
@@ -223,7 +279,7 @@
     projected = lax.fori_loop(
         0, width // CHUNK, part, jnp.zeros((tokens, rank), jnp.float32)
     ).astype(jnp.bfloat16)
-    g_up = scale * dot(projected, up_ref[...], (0, 0))
+    g_up = scale * dot(projected, up_all[o], (0, 0))
     for j in range(per_up):
         grad[pl.ds(down_rows + j, rank, stride=per_up), :] = g_up[:, j * LANES : (j + 1) * LANES]
 
@@ -234,7 +290,6 @@
 
     g_core_far = send(grad.at[grad_rows(o_diag)], from_core.at[0], core_dev)
     g_core_own = send(grad.at[grad_rows(o_core)], from_core.at[1], core_dev)
-    pass_weight(1)
     u_core.wait_recv()
     u_far.wait_recv()
     u_rows = 4 * tokens
@@ -242,21 +297,30 @@
 
     block_copies = []
 
-    def block_math(k):
-        first = pl.multiple_of((o * 4 + z_from[k]) * feats, feats)
-        w = w_ref[...] if k == 0 else w_buf[k - 1]
-        value = dot(up_all[...].reshape(u_rows, value_width), w, (1, 1)) + scale * dot(
-            rank_all, down[:, pl.ds(first, feats)], (1, 0)
-        )
-        blocks[k] = value.astype(jnp.bfloat16).reshape(4, tokens, feats)
-        out_ref[:, pl.ds(first, feats)] = blocks[k, o]
-
-    def block_send(k):
-        first = pl.multiple_of((o * 4 + z_from[k]) * feats, feats)
+    def block_cols(n):
+        return pl.ds(pl.multiple_of((o * 4 + order[n]) * feats, feats), feats)
+
+    def block_math(n):
+        cols = block_cols(n)
+        value = dot(up_all[...].reshape(u_rows, value_width), w_buf[order[n]], (1, 1))
+        value += scale * dot(rank_all, down[:, cols], (1, 0))
+        blocks[n] = value.astype(jnp.bfloat16).reshape(4, tokens, feats)
+        out_ref[:, cols] = blocks[n, o]
+
+    def block_send(n):
         for to, device in ((o_x, x_dev), (o_diag, diag_dev), (o_core, core_dev)):
-            block_copies.append(
-                send(blocks.at[k, to], out_ref.at[:, pl.ds(first, feats)], device)
-            )
+            block_copies.append(send(blocks.at[n, to], out_ref.at[:, block_cols(n)], device))
+
+    def weight_ready(n):
+        b = order[n]
+        pltpu.make_async_remote_copy(
+            src_ref=w_buf.at[b, other_half],
+            dst_ref=w_buf.at[b, other_half],
+            send_sem=w_send_sem.at[2, b],
+            recv_sem=w_recv_sem.at[1, b],
+            device_id=y_dev,
+            device_id_type=MESH,
+        ).wait_recv()
 
     block_math(0)
     g_core_far.wait_recv()
@@ -265,8 +329,9 @@
     block_send(0)
     g_core_own.wait_recv()
     half_sum[1] = grad[grad_rows(o), :] + from_core[1]
-    pass_weight(2)
-    w_y[1].wait_recv()
+    pl.when(middle)(lambda: arrive(3))
+    pl.when(jnp.logical_not(middle))(lambda: arrive(2))
+    weight_ready(1)
     block_math(1)
     block_send(1)
     g_x.wait_recv()
@@ -278,17 +343,17 @@
     g_z = [
         send(half_sum.at[1, shard(z_to[k])], from_z.at[k - 1], z_devs[k]) for k in range(1, 4)
     ]
-    pass_weight(3)
-    w_y[2].wait_recv()
+    pl.when(jnp.logical_not(middle))(lambda: arrive(3))
+    weight_ready(2)
     block_math(2)
     block_send(2)
     for copy in g_z:
         copy.wait_recv()
     total = half_sum[1, shard(z), :] + from_z[0] + from_z[1] + from_z[2]
-    grad_total = total
+    clipped_ref[...] = total
     sq_own[...] = jnp.sum((total * total).reshape(shard_rows // 8, 8, LANES), axis=0)
     s_z = [send(sq_own, sq_z.at[k - 1], z_devs[k]) for k in range(1, 4)]
-    w_y[3].wait_recv()
+    weight_ready(3)
     block_math(3)
     block_send(3)
     for copy in s_z:
@@ -301,13 +366,18 @@
     for copy in s_s:
         copy.wait_recv()
     sum_squares = jnp.sum(sq_line[...] + sq_s[0] + sq_s[1] + sq_s[2], keepdims=True)
-    new_master_ref[...], new_moment_ref[...], new_second_ref[...] = adam(
-        grad_total, sum_squares, master_ref[...], moment_ref[...], second_ref[...], params
-    )
+    norm = jnp.sqrt(sum_squares + 1e-06)
+    clipped_ref[...] = clipped_ref[...] * jnp.minimum(1.0, math.sqrt(params) / norm)
     for copy in block_copies:
         copy.wait_recv()
     for copy in used:
         copy.wait_send()
+    for n in range(4):
+        b = order[n]
+        pl.when(goes_up(b))(lambda b=b: weight_up(b).wait_send())
+        pl.when(goes_down(b))(lambda b=b: weight_down(b).wait_send())
+        if n > 0:
+            weight_y(b).wait_send()
 
 
 N_COPIES = 64
@@ -323,17 +393,20 @@
     state = jax.ShapeDtypeStruct((shard_rows, LANES), jnp.float32)
     bf16, f32 = jnp.bfloat16, jnp.float32
     vmem = pl.BlockSpec(memory_space=pltpu.VMEM)
-    result = pl.pallas_call(
+    hbm = pl.BlockSpec(memory_space=pltpu.HBM)
+    rows, clipped = pl.pallas_call(
         functools.partial(kernel, rank),
-        out_shape=(jax.ShapeDtypeStruct((tokens, width), bf16), state, state, state),
-        in_specs=[vmem] * 6,
-        out_specs=(vmem,) * 4,
+        out_shape=(jax.ShapeDtypeStruct((tokens, width), bf16), state),
+        in_specs=[hbm] * 4,
+        out_specs=(vmem,) * 2,
         scratch_shapes=[
+            pltpu.VMEM((tokens, width), bf16),
+            pltpu.VMEM((shard_rows, LANES), f32),
             pltpu.VMEM((16, padded, LANES), bf16),
             pltpu.VMEM((flat_rows, LANES), f32),
             pltpu.VMEM((rank, width), bf16),
             pltpu.VMEM((4, tokens, value_width), bf16),
-            pltpu.VMEM((3, feats, value_width), bf16),
+            pltpu.VMEM((4, feats, value_width), bf16),
             pltpu.VMEM((flat_rows, LANES), f32),
             pltpu.VMEM((2, 4 * shard_rows, LANES), f32),
             pltpu.VMEM((2, 4 * shard_rows, LANES), f32),
@@ -344,22 +417,18 @@
             pltpu.VMEM((8, LANES), f32),
             pltpu.VMEM((3, 8, LANES), f32),
             pltpu.VMEM((4, 4, tokens, feats), bf16),
+            pltpu.SemaphoreType.DMA((4,)),
             pltpu.SemaphoreType.DMA((N_COPIES,)),
             pltpu.SemaphoreType.DMA((N_COPIES,)),
+            pltpu.SemaphoreType.DMA((3, 4)),
+            pltpu.SemaphoreType.DMA((2, 4)),
         ],
         compiler_params=pltpu.CompilerParams(
-            collective_id=0, has_side_effects=True, vmem_limit_bytes=52 * 1024 * 1024
+            collective_id=0, has_side_effects=True, vmem_limit_bytes=56 * 1024 * 1024
         ),
         name="adapter_backward",
-    )(
-        activations,
-        upstream,
-        weight,
-        master.reshape(shard_rows, LANES),
-        moment.reshape(shard_rows, LANES),
-        second_moment.reshape(shard_rows, LANES),
-    )
-    return (result[0],) + tuple(r.reshape(-1) for r in result[1:])
+    )(activations, upstream, weight, master.reshape(shard_rows, LANES))
+    return (rows,) + adam(clipped.reshape(-1), master, moment, second_moment)
 
 
 def solution(mesh):

time: 89.9 us -> 71.1 us (0.79)
  Pallas kernels: 78.8 us -> 65.4 us
  local copies, waits for them, and re-layouts: 9.88 us -> 3.11 us
  other arithmetic: 0 us -> 1.72 us
    pallas_call x1, Pallas kernels: 78.8 us -> 65.4 us  [fused(): pl.pallas_call(functools.partial(kernel, rank), out_shape=(jax.ShapeDtype...]
    unnamed x14 -> x7, local copies, waits for them, and re-layouts: 9.88 us -> 3.11 us
    sub x0 -> x1, other arithmetic: none -> 1.72 us  [adam(): master - 0.1 * (new_moment / corr_one) / (jnp.sqrt(new_second / corr_two)...]
where the time goes in v2:
time: 71.1 us; the launch traced here: 71 us
  Pallas kernels  65.4 us (92%)
  local copies, waits for them, and re-layouts  3.11 us (4%)
  other arithmetic  1.72 us (2%)
    pallas_call x1, Pallas kernels, fused(): pl.pallas_call(functools.partial(kernel, rank), out_shape=(jax.ShapeDtype...  65.4 us
    unnamed x7, local copies, waits for them, and re-layouts  3.11 us
    sub x1, other arithmetic, adam(): master - 0.1 * (new_moment / corr_one) / (jnp.sqrt(new_second / corr_two)...  1.72 us

profile of v2, /device:TPU:0, one launch (start us, length us, event | category | flops | bytes accessed | tf_op | source)
XLA Modules:
  0.0 71.0 jit_solution(14517927743630310431)
XLA Ops:
  0.6 0.0 copy-start
  0.6 0.0 copy-start.2
  0.7 0.0 copy-start.1
  0.7 65.4 %adapter_backward.1 = (bf16[128,8192]{1,0:T(8,128)(2,1)}, f32[280,128]{1,0:T(8,128)}) custom-call(bf16[128,8192]{1,0:T(8,128)(2,1)} %act_hbm.1, bf16[128,768]{1,0:T(8,128)(2,1)} %up_hbm.1, bf16[512,768]{1,0:T(8,128)(2,1)} %w_hbm.1, f32[280,128]{1,0:T(8,128)} %bitcast.8), custom_call_target="tpu_custom_call" | custom-call | tf_op jit(solution)/shard_map/adapter_backward/pallas_call | solution.py:397
  66.1 0.0 copy-done
  66.1 0.0 copy-done.2
  66.1 0.0 copy-done.1
  66.1 1.7 %divide_subtract_fusion = (f32[35840]{0:T(1024)}, f32[35840]{0:T(1024)}, f32[35840]{0:T(1024)}) fusion(f32[35840]{0:T(1024)S(1)} %copy-done, f32[280,128]{1,0:T(8,128)} %get-tuple-element.7, f32[35840]{0:T(1024)S(1)} %copy-done.1, f32[35840]{0:T(1024)S(1)} %copy-done.2), kind=kLoop, calls=%fused_computation.4 | loop fusion | flops 430080 | bytes 1003520 | tf_op jit(solution)/shard_map/sub | solution.py:79
  67.9 3.1 %copy.11 = bf16[128,8192]{1,0:T(8,128)(2,1)} copy(bf16[128,8192]{1,0:T(8,128)(2,1)} %get-tuple-element.15) | data formatting | bytes 4194304
Async XLA Ops:
  0.6 65.5 %copy-start = (f32[35840]{0:T(1024)S(1)}, f32[35840]{0:T(1024)}, u32[]{:S(2)}) copy-start(f32[35840]{0:T(1024)} %param.9) | copy-start | bytes 430084
  0.6 65.5 %copy-start.2 = (f32[35840]{0:T(1024)S(1)}, f32[35840]{0:T(1024)}, u32[]{:S(2)}) copy-start(f32[35840]{0:T(1024)} %param.11) | copy-start | bytes 430084
  0.7 65.5 %copy-start.1 = (f32[35840]{0:T(1024)S(1)}, f32[35840]{0:T(1024)}, u32[]{:S(2)}) copy-start(f32[35840]{0:T(1024)} %param.10) | copy-start | bytes 430084

commit v3 on v2

--- a/solution.py
+++ b/solution.py
@@ -232,8 +232,6 @@
     slot_z = [None] + [send(slots.at[own], slots.at[own], z_devs[k]) for k in range(1, 4)]
     slot_x = [send(slots.at[own], slots.at[own], x_dev)]
     slot_core = [send(slots.at[own], slots.at[own], core_dev)]
-    load_w.wait()
-    pass_on(z)
     load_up.wait()
     u_x = send(up_all.at[o], up_all.at[o], x_dev)
     u_core = send(up_all.at[o], up_all.at[o], core_dev)
@@ -242,16 +240,14 @@
         at = slots.at[o * 4 + z_from[k]]
         slot_x.append(send(at, at, x_dev))
         slot_core.append(send(at, at, core_dev))
+    load_w.wait()
+    pass_on(z)
     for k in range(4):
         slot_x[k].wait_recv()
         at = slots.at[o_x * 4 + z_from[k]]
         slot_core.append(send(at, at, core_dev))
     u_x.wait_recv()
     u_far = send(up_all.at[o_x], up_all.at[o_x], core_dev)
-    middle = u == 1
-    arrive(1)
-    pl.when(middle)(lambda: arrive(2))
-
     for copy in slot_core:
         copy.wait_recv()
     for d in range(16):
@@ -261,35 +257,11 @@
     up_m = jnp.concatenate(
         [flat[pl.ds(down_rows + j, rank, stride=per_up), :] for j in range(per_up)], axis=1
     ).astype(jnp.bfloat16)
-    own_rank = dot(up_all[o], up_m, (1, 1)).astype(jnp.bfloat16)
     per_row = width // LANES
-    load_act.wait()
-
-    def part(n, projected):
-        cols = pl.ds(pl.multiple_of(n * CHUNK, CHUNK), CHUNK)
-        rows = [pl.ds(n * (CHUNK // LANES) + j, rank, stride=per_row) for j in range(CHUNK // LANES)]
-        d_part = jnp.concatenate([flat[r, :] for r in rows], axis=1).astype(jnp.bfloat16)
-        down[:, cols] = d_part
-        a_part = act_ref[:, cols]
-        g_part = scale * dot(own_rank, a_part, (0, 0))
-        for j, r in enumerate(rows):
-            grad[r, :] = g_part[:, j * LANES : (j + 1) * LANES]
-        return projected + dot(a_part, d_part, (1, 1))
-
-    projected = lax.fori_loop(
-        0, width // CHUNK, part, jnp.zeros((tokens, rank), jnp.float32)
-    ).astype(jnp.bfloat16)
-    g_up = scale * dot(projected, up_all[o], (0, 0))
-    for j in range(per_up):
-        grad[pl.ds(down_rows + j, rank, stride=per_up), :] = g_up[:, j * LANES : (j + 1) * LANES]
-
-    quarter = 4 * shard_rows
-
-    def grad_rows(at):
-        return pl.ds(pl.multiple_of(at * quarter, quarter), quarter)
-
-    g_core_far = send(grad.at[grad_rows(o_diag)], from_core.at[0], core_dev)
-    g_core_own = send(grad.at[grad_rows(o_core)], from_core.at[1], core_dev)
+    for j in range(per_row):
+        row = flat[pl.ds(j, rank, stride=per_row), :]
+        down[:, j * LANES : (j + 1) * LANES] = row.astype(jnp.bfloat16)
+
     u_core.wait_recv()
     u_far.wait_recv()
     u_rows = 4 * tokens
@@ -323,17 +295,46 @@
         ).wait_recv()
 
     block_math(0)
+    block_send(0)
+
+    own_rank_t = jnp.transpose(dot(up_all[o], up_m, (1, 1))).astype(jnp.bfloat16)
+    load_act.wait()
+
+    def part(n, projected):
+        cols = pl.ds(pl.multiple_of(n * CHUNK, CHUNK), CHUNK)
+        a_part = act_ref[:, cols]
+        g_part = scale * dot(own_rank_t, a_part, (1, 0))
+        for j in range(CHUNK // LANES):
+            at = pl.ds(n * (CHUNK // LANES) + j, rank, stride=per_row)
+            grad[at, :] = g_part[:, j * LANES : (j + 1) * LANES]
+        return projected + dot(a_part, down[:, cols], (1, 1))
+
+    projected = lax.fori_loop(
+        0, width // CHUNK, part, jnp.zeros((tokens, rank), jnp.float32)
+    ).astype(jnp.bfloat16)
+    g_up = scale * dot(projected, up_all[o], (0, 0))
+    for j in range(per_up):
+        grad[pl.ds(down_rows + j, rank, stride=per_up), :] = g_up[:, j * LANES : (j + 1) * LANES]
+
+    quarter = 4 * shard_rows
+
+    def grad_rows(at):
+        return pl.ds(pl.multiple_of(at * quarter, quarter), quarter)
+
+    g_core_far = send(grad.at[grad_rows(o_diag)], from_core.at[0], core_dev)
+    g_core_own = send(grad.at[grad_rows(o_core)], from_core.at[1], core_dev)
+    middle = u == 1
     g_core_far.wait_recv()
     half_sum[0] = grad[grad_rows(o_x), :] + from_core[0]
     g_x = send(half_sum.at[0], from_x, x_dev)
-    block_send(0)
+    arrive(1)
+    pl.when(middle)(lambda: arrive(2))
     g_core_own.wait_recv()
     half_sum[1] = grad[grad_rows(o), :] + from_core[1]
     pl.when(middle)(lambda: arrive(3))
     pl.when(jnp.logical_not(middle))(lambda: arrive(2))
     weight_ready(1)
     block_math(1)
-    block_send(1)
     g_x.wait_recv()
     half_sum[1] += from_x[...]
 
@@ -343,6 +344,7 @@
     g_z = [
         send(half_sum.at[1, shard(z_to[k])], from_z.at[k - 1], z_devs[k]) for k in range(1, 4)
     ]
+    block_send(1)
     pl.when(jnp.logical_not(middle))(lambda: arrive(3))
     weight_ready(2)
     block_math(2)

time: 71.1 us -> 74.1 us (1.042)
  Pallas kernels: 65.4 us -> 68.4 us
    pallas_call x1, Pallas kernels: 65.4 us -> 68.4 us  [fused(): pl.pallas_call(functools.partial(kernel, rank), out_shape=(jax.ShapeDtype...]
where the time goes in v3:
time: 74.1 us; the launch traced here: 73.9 us
  Pallas kernels  68.4 us (92%)
  local copies, waits for them, and re-layouts  3.11 us (4%)
  other arithmetic  1.72 us (2%)
    pallas_call x1, Pallas kernels, fused(): pl.pallas_call(functools.partial(kernel, rank), out_shape=(jax.ShapeDtype...  68.4 us
    unnamed x7, local copies, waits for them, and re-layouts  3.11 us
    sub x1, other arithmetic, adam(): master - 0.1 * (new_moment / corr_one) / (jnp.sqrt(new_second / corr_two)...  1.72 us

profile of v3, /device:TPU:0, one launch (start us, length us, event | category | flops | bytes accessed | tf_op | source)
XLA Modules:
  0.0 73.9 jit_solution(7764783555546495227)
XLA Ops:
  0.6 0.0 copy-start
  0.6 0.0 copy-start.2
  0.7 0.0 copy-start.1
  0.7 68.4 %adapter_backward.1 = (bf16[128,8192]{1,0:T(8,128)(2,1)}, f32[280,128]{1,0:T(8,128)}) custom-call(bf16[128,8192]{1,0:T(8,128)(2,1)} %act_hbm.1, bf16[128,768]{1,0:T(8,128)(2,1)} %up_hbm.1, bf16[512,768]{1,0:T(8,128)(2,1)} %w_hbm.1, f32[280,128]{1,0:T(8,128)} %bitcast.8), custom_call_target="tpu_custom_call" | custom-call | tf_op jit(solution)/shard_map/adapter_backward/pallas_call | solution.py:399
  69.1 0.0 copy-done
  69.1 0.0 copy-done.2
  69.1 0.0 copy-done.1
  69.1 1.7 %divide_subtract_fusion = (f32[35840]{0:T(1024)}, f32[35840]{0:T(1024)}, f32[35840]{0:T(1024)}) fusion(f32[35840]{0:T(1024)S(1)} %copy-done, f32[280,128]{1,0:T(8,128)} %get-tuple-element.7, f32[35840]{0:T(1024)S(1)} %copy-done.1, f32[35840]{0:T(1024)S(1)} %copy-done.2), kind=kLoop, calls=%fused_computation.4 | loop fusion | flops 430080 | bytes 1003520 | tf_op jit(solution)/shard_map/sub | solution.py:79
  70.8 3.1 %copy.11 = bf16[128,8192]{1,0:T(8,128)(2,1)} copy(bf16[128,8192]{1,0:T(8,128)(2,1)} %get-tuple-element.15) | data formatting | bytes 4194304
Async XLA Ops:
  0.6 68.4 %copy-start = (f32[35840]{0:T(1024)S(1)}, f32[35840]{0:T(1024)}, u32[]{:S(2)}) copy-start(f32[35840]{0:T(1024)} %param.9) | copy-start | bytes 430084
  0.6 68.4 %copy-start.2 = (f32[35840]{0:T(1024)S(1)}, f32[35840]{0:T(1024)}, u32[]{:S(2)}) copy-start(f32[35840]{0:T(1024)} %param.11) | copy-start | bytes 430084
  0.7 68.4 %copy-start.1 = (f32[35840]{0:T(1024)S(1)}, f32[35840]{0:T(1024)}, u32[]{:S(2)}) copy-start(f32[35840]{0:T(1024)} %param.10) | copy-start | bytes 430084

commit v4 on v3

--- a/solution.py
+++ b/solution.py
@@ -11,6 +11,9 @@
 MESH = pl.DeviceIdType.MESH
 LANES = 128
 CHUNK = 1024
+PIECES = 2
+ROW_COPIES = 8
+VMEM_GRANT = 56 * 1024 * 1024
 
 
 def per_device(activations, upstream, frozen_weight_matrix, master, moment, second_moment):
@@ -98,7 +101,6 @@
     master_ref,
     slots,
     flat,
-    down,
     up_all,
     w_buf,
     grad,
@@ -186,48 +188,57 @@
     ).astype(jnp.bfloat16)
     pl.semaphore_wait(barrier, len(partners))
 
-    my_half = pl.ds(pl.multiple_of(y * half, half), half)
-    other_half = pl.ds(pl.multiple_of((1 - y) * half, half), half)
-
-    def weight_copy(b, way, device):
-        at = w_buf.at[b, my_half]
+    piece = half // PIECES
+
+    def weight_rows(part_y, m):
+        return pl.ds(pl.multiple_of(part_y * half + m * piece, piece), piece)
+
+    def weight_copy(b, m, part_y, way, device):
+        at = w_buf.at[b, weight_rows(part_y, m)]
         return pltpu.make_async_remote_copy(
             src_ref=at,
             dst_ref=at,
-            send_sem=w_send_sem.at[way, b],
-            recv_sem=w_recv_sem.at[way // 2, b],
+            send_sem=w_send_sem.at[way, m, b],
+            recv_sem=w_recv_sem.at[way // 2, m, b],
             device_id=device,
             device_id_type=MESH,
         )
 
-    def weight_up(b):
-        return weight_copy(b, 0, {"inner": z + 1})
-
-    def weight_down(b):
-        return weight_copy(b, 1, {"inner": z - 1})
-
-    def weight_y(b):
-        return weight_copy(b, 2, y_dev)
+    def weight_up(b, m):
+        return weight_copy(b, m, y, 0, {"inner": z + 1})
+
+    def weight_down(b, m):
+        return weight_copy(b, m, y, 1, {"inner": z - 1})
+
+    def weight_y(b, m):
+        return weight_copy(b, m, y, 2, y_dev)
 
     goes_up = lambda b: (b <= z) & (z < 3)
     goes_down = lambda b: (b >= z) & (z > 0)
 
-    def pass_on(b):
-        pl.when(goes_up(b))(lambda: weight_up(b).start())
-        pl.when(goes_down(b))(lambda: weight_down(b).start())
-
-    def arrive(n):
+    def pass_on(b, m):
+        pl.when(goes_up(b))(lambda: weight_up(b, m).start())
+        pl.when(goes_down(b))(lambda: weight_down(b, m).start())
+
+    def arrive(n, m):
         b = order[n]
-        pltpu.make_async_remote_copy(
-            src_ref=w_buf.at[b, my_half],
-            dst_ref=w_buf.at[b, my_half],
-            send_sem=w_send_sem.at[0, b],
-            recv_sem=w_recv_sem.at[0, b],
-            device_id=y_dev,
-            device_id_type=MESH,
-        ).wait_recv()
-        pass_on(b)
-        weight_y(b).start()
+        weight_copy(b, m, y, 0, y_dev).wait_recv()
+        pass_on(b, m)
+        weight_y(b, m).start()
+
+    def weight_ready(n):
+        for m in range(PIECES):
+            weight_copy(order[n], m, 1 - y, 2, y_dev).wait_recv()
+
+    middle = u == 1
+
+    def arrive_early(n, m):
+        pl.when(middle)(lambda: arrive(n + 1, m))
+        pl.when(jnp.logical_not(middle))(lambda: arrive(n, m))
+
+    def to_flat(d):
+        at = pl.ds(pl.multiple_of(d * shard_rows, shard_rows), shard_rows)
+        flat[at, :] = slots[d].astype(jnp.float32)[:shard_rows]
 
     slot_z = [None] + [send(slots.at[own], slots.at[own], z_devs[k]) for k in range(1, 4)]
     slot_x = [send(slots.at[own], slots.at[own], x_dev)]
@@ -241,26 +252,31 @@
         slot_x.append(send(at, at, x_dev))
         slot_core.append(send(at, at, core_dev))
     load_w.wait()
-    pass_on(z)
+    for m in range(PIECES):
+        pass_on(z, m)
+    for k in range(4):
+        to_flat(o * 4 + z_from[k])
     for k in range(4):
         slot_x[k].wait_recv()
         at = slots.at[o_x * 4 + z_from[k]]
         slot_core.append(send(at, at, core_dev))
     u_x.wait_recv()
     u_far = send(up_all.at[o_x], up_all.at[o_x], core_dev)
-    for copy in slot_core:
-        copy.wait_recv()
-    for d in range(16):
-        flat[d * shard_rows : (d + 1) * shard_rows, :] = slots[d].astype(jnp.float32)[:shard_rows]
+    for k in range(4):
+        to_flat(o_x * 4 + z_from[k])
+    for k in range(8):
+        slot_core[k].wait_recv()
+        to_flat((o_core if k < 4 else o_diag) * 4 + z_from[k % 4])
 
     per_up = value_width // LANES
     up_m = jnp.concatenate(
         [flat[pl.ds(down_rows + j, rank, stride=per_up), :] for j in range(per_up)], axis=1
     ).astype(jnp.bfloat16)
     per_row = width // LANES
-    for j in range(per_row):
-        row = flat[pl.ds(j, rank, stride=per_row), :]
-        down[:, j * LANES : (j + 1) * LANES] = row.astype(jnp.bfloat16)
+
+    def down_part(first, count):
+        rows = [flat[pl.ds(first + j, rank, stride=per_row), :] for j in range(count)]
+        return jnp.concatenate(rows, axis=1).astype(jnp.bfloat16)
 
     u_core.wait_recv()
     u_far.wait_recv()
@@ -274,8 +290,10 @@
 
     def block_math(n):
         cols = block_cols(n)
+        per_block = feats // LANES
+        d_block = down_part((o * 4 + order[n]) * per_block, per_block)
         value = dot(up_all[...].reshape(u_rows, value_width), w_buf[order[n]], (1, 1))
-        value += scale * dot(rank_all, down[:, cols], (1, 0))
+        value += scale * dot(rank_all, d_block, (1, 0))
         blocks[n] = value.astype(jnp.bfloat16).reshape(4, tokens, feats)
         out_ref[:, cols] = blocks[n, o]
 
@@ -283,19 +301,10 @@
         for to, device in ((o_x, x_dev), (o_diag, diag_dev), (o_core, core_dev)):
             block_copies.append(send(blocks.at[n, to], out_ref.at[:, block_cols(n)], device))
 
-    def weight_ready(n):
-        b = order[n]
-        pltpu.make_async_remote_copy(
-            src_ref=w_buf.at[b, other_half],
-            dst_ref=w_buf.at[b, other_half],
-            send_sem=w_send_sem.at[2, b],
-            recv_sem=w_recv_sem.at[1, b],
-            device_id=y_dev,
-            device_id_type=MESH,
-        ).wait_recv()
-
     block_math(0)
     block_send(0)
+    arrive(1, 0)
+    pl.when(middle)(lambda: arrive(2, 0))
 
     own_rank_t = jnp.transpose(dot(up_all[o], up_m, (1, 1))).astype(jnp.bfloat16)
     load_act.wait()
@@ -307,7 +316,7 @@
         for j in range(CHUNK // LANES):
             at = pl.ds(n * (CHUNK // LANES) + j, rank, stride=per_row)
             grad[at, :] = g_part[:, j * LANES : (j + 1) * LANES]
-        return projected + dot(a_part, down[:, cols], (1, 1))
+        return projected + dot(a_part, down_part(n * (CHUNK // LANES), CHUNK // LANES), (1, 1))
 
     projected = lax.fori_loop(
         0, width // CHUNK, part, jnp.zeros((tokens, rank), jnp.float32)
@@ -323,18 +332,21 @@
 
     g_core_far = send(grad.at[grad_rows(o_diag)], from_core.at[0], core_dev)
     g_core_own = send(grad.at[grad_rows(o_core)], from_core.at[1], core_dev)
-    middle = u == 1
+    arrive(1, 1)
+    pl.when(middle)(lambda: arrive(2, 1))
     g_core_far.wait_recv()
     half_sum[0] = grad[grad_rows(o_x), :] + from_core[0]
     g_x = send(half_sum.at[0], from_x, x_dev)
-    arrive(1)
-    pl.when(middle)(lambda: arrive(2))
+    arrive_early(2, 0)
     g_core_own.wait_recv()
     half_sum[1] = grad[grad_rows(o), :] + from_core[1]
-    pl.when(middle)(lambda: arrive(3))
-    pl.when(jnp.logical_not(middle))(lambda: arrive(2))
+    arrive_early(2, 1)
     weight_ready(1)
     block_math(1)
+    pl.when(jnp.logical_not(middle))(lambda: arrive(3, 0))
+    weight_ready(2)
+    block_math(2)
+    pl.when(jnp.logical_not(middle))(lambda: arrive(3, 1))
     g_x.wait_recv()
     half_sum[1] += from_x[...]
 
@@ -345,19 +357,16 @@
         send(half_sum.at[1, shard(z_to[k])], from_z.at[k - 1], z_devs[k]) for k in range(1, 4)
     ]
     block_send(1)
-    pl.when(jnp.logical_not(middle))(lambda: arrive(3))
-    weight_ready(2)
-    block_math(2)
     block_send(2)
+    weight_ready(3)
+    block_math(3)
+    block_send(3)
     for copy in g_z:
         copy.wait_recv()
     total = half_sum[1, shard(z), :] + from_z[0] + from_z[1] + from_z[2]
     clipped_ref[...] = total
     sq_own[...] = jnp.sum((total * total).reshape(shard_rows // 8, 8, LANES), axis=0)
     s_z = [send(sq_own, sq_z.at[k - 1], z_devs[k]) for k in range(1, 4)]
-    weight_ready(3)
-    block_math(3)
-    block_send(3)
     for copy in s_z:
         copy.wait_recv()
     sq_line[...] = sq_own[...] + sq_z[0] + sq_z[1] + sq_z[2]
@@ -375,11 +384,37 @@
     for copy in used:
         copy.wait_send()
     for n in range(4):
-        b = order[n]
-        pl.when(goes_up(b))(lambda b=b: weight_up(b).wait_send())
-        pl.when(goes_down(b))(lambda b=b: weight_down(b).wait_send())
-        if n > 0:
-            weight_y(b).wait_send()
+        for m in range(PIECES):
+            b = order[n]
+            pl.when(goes_up(b))(lambda b=b, m=m: weight_up(b, m).wait_send())
+            pl.when(goes_down(b))(lambda b=b, m=m: weight_down(b, m).wait_send())
+            if n > 0:
+                weight_y(b, m).wait_send()
+
+
+def finish(
+    rows_in,
+    clipped_ref,
+    master_ref,
+    moment_ref,
+    second_ref,
+    rows_out,
+    new_master_ref,
+    new_moment_ref,
+    new_second_ref,
+    sem,
+):
+    step = rows_in.shape[0] // ROW_COPIES
+    copies = []
+    for n in range(ROW_COPIES):
+        at = pl.ds(n * step, step)
+        copies.append(pltpu.make_async_copy(rows_in.at[at], rows_out.at[at], sem.at[n]))
+        copies[-1].start()
+    new_master_ref[...], new_moment_ref[...], new_second_ref[...] = adam(
+        clipped_ref[...], master_ref[...], moment_ref[...], second_ref[...]
+    )
+    for copy in copies:
+        copy.wait()
 
 
 N_COPIES = 64
@@ -406,7 +441,6 @@
             pltpu.VMEM((shard_rows, LANES), f32),
             pltpu.VMEM((16, padded, LANES), bf16),
             pltpu.VMEM((flat_rows, LANES), f32),
-            pltpu.VMEM((rank, width), bf16),
             pltpu.VMEM((4, tokens, value_width), bf16),
             pltpu.VMEM((4, feats, value_width), bf16),
             pltpu.VMEM((flat_rows, LANES), f32),
@@ -422,15 +456,30 @@
             pltpu.SemaphoreType.DMA((4,)),
             pltpu.SemaphoreType.DMA((N_COPIES,)),
             pltpu.SemaphoreType.DMA((N_COPIES,)),
-            pltpu.SemaphoreType.DMA((3, 4)),
-            pltpu.SemaphoreType.DMA((2, 4)),
+            pltpu.SemaphoreType.DMA((3, PIECES, 4)),
+            pltpu.SemaphoreType.DMA((2, PIECES, 4)),
         ],
         compiler_params=pltpu.CompilerParams(
-            collective_id=0, has_side_effects=True, vmem_limit_bytes=56 * 1024 * 1024
+            collective_id=0, has_side_effects=True, vmem_limit_bytes=VMEM_GRANT
         ),
         name="adapter_backward",
     )(activations, upstream, weight, master.reshape(shard_rows, LANES))
-    return (rows,) + adam(clipped.reshape(-1), master, moment, second_moment)
+    result = pl.pallas_call(
+        finish,
+        out_shape=(jax.ShapeDtypeStruct((tokens, width), bf16), state, state, state),
+        in_specs=[hbm] + [vmem] * 4,
+        out_specs=(hbm,) + (vmem,) * 3,
+        scratch_shapes=[pltpu.SemaphoreType.DMA((ROW_COPIES,))],
+        compiler_params=pltpu.CompilerParams(vmem_limit_bytes=VMEM_GRANT),
+        name="finish",
+    )(
+        rows,
+        clipped,
+        master.reshape(shard_rows, LANES),
+        moment.reshape(shard_rows, LANES),
+        second_moment.reshape(shard_rows, LANES),
+    )
+    return (result[0],) + tuple(r.reshape(-1) for r in result[1:])
 
 
 def solution(mesh):
@@ -441,7 +490,7 @@
         width, value_width = activations.shape[1], upstream.shape[1]
         rank = master.shape[0] * sizes["outer"] * sizes["inner"] // (width + value_width)
         fits = (
-            activations.shape[0] % 16 == 0
+            activations.shape[0] % (16 * ROW_COPIES) == 0
             and width % CHUNK == 0
             and value_width % LANES == 0
             and weight.shape[0] % 256 == 0

time: 74.1 us -> 131 us (1.77)
  Pallas kernels: 68.4 us -> 130 us
  local copies, waits for them, and re-layouts: 3.11 us -> 0 us
  other arithmetic: 1.72 us -> 0 us
    pallas_call x0 -> x1, Pallas kernels: none -> 66.6 us  [fused(): pl.pallas_call(finish, out_shape=(jax.ShapeDtypeStruct((tokens, width), b...]
    pallas_call x1, Pallas kernels: 68.4 us -> 63.6 us  [fused(): pl.pallas_call(functools.partial(kernel, rank), out_shape=(jax.ShapeDtype...]
    unnamed x7 -> x0, local copies, waits for them, and re-layouts: 3.11 us -> none
    sub x1 -> x0, other arithmetic: 1.72 us -> none  [adam(): master - 0.1 * (new_moment / corr_one) / (jnp.sqrt(new_second / corr_two)...]
where the time goes in v4:
time: 131 us
  Pallas kernels  130 us (99%)
    pallas_call x1, Pallas kernels, fused(): pl.pallas_call(finish, out_shape=(jax.ShapeDtypeStruct((tokens, width), b...  66.6 us
    pallas_call x1, Pallas kernels, fused(): pl.pallas_call(functools.partial(kernel, rank), out_shape=(jax.ShapeDtype...  63.6 us

profile of v4, /device:TPU:0, one launch (start us, length us, event | category | flops | bytes accessed | tf_op | source)
XLA Modules:
  0.0 130.8 jit_solution(12947133988119130271)
XLA Ops:
  0.6 63.6 %adapter_backward.1 = (bf16[128,8192]{1,0:T(8,128)(2,1)}, f32[280,128]{1,0:T(8,128)}) custom-call(bf16[128,8192]{1,0:T(8,128)(2,1)} %act_hbm.1, bf16[128,768]{1,0:T(8,128)(2,1)} %up_hbm.1, bf16[512,768]{1,0:T(8,128)(2,1)} %w_hbm.1, f32[280,128]{1,0:T(8,128)} %bitcast.6), custom_call_target="tpu_custom_call" | custom-call | tf_op jit(solution)/shard_map/adapter_backward/pallas_call | solution.py:434
  64.2 66.6 %finish.1 = (bf16[128,8192]{1,0:T(8,128)(2,1)}, f32[280,128]{1,0:T(8,128)}, f32[280,128]{1,0:T(8,128)}, f32[280,128]{1,0:T(8,128)}) custom-call(bf16[128,8192]{1,0:T(8,128)(2,1)} %get-tuple-element.10.rows_in, f32[280,128]{1,0:T(8,128)} %get-tuple-element.11.clipped_ref, f32[280,128]{1,0:T(8,128)} %bitcast.7, f32[280,128]{1,0:T(8,128)} %bitcast.8, ...), custom_call_target="tpu_custom_call" | custom-call | tf_op jit(solution)/shard_map/finish/pallas_call | solution.py:467

commit v5 on v4

--- a/solution.py
+++ b/solution.py
@@ -12,7 +12,7 @@
 LANES = 128
 CHUNK = 1024
 PIECES = 2
-ROW_COPIES = 8
+ROW_COPIES = 4
 VMEM_GRANT = 56 * 1024 * 1024
 
 
@@ -118,6 +118,8 @@
     recv_sem,
     w_send_sem,
     w_recv_sem,
+    shard_send_sem,
+    shard_recv_sem,
 ):
     y = lax.axis_index("groups")
     o = lax.axis_index("outer")
@@ -321,49 +323,69 @@
     projected = lax.fori_loop(
         0, width // CHUNK, part, jnp.zeros((tokens, rank), jnp.float32)
     ).astype(jnp.bfloat16)
+    arrive(1, 1)
+    pl.when(middle)(lambda: arrive(2, 1))
     g_up = scale * dot(projected, up_all[o], (0, 0))
     for j in range(per_up):
         grad[pl.ds(down_rows + j, rank, stride=per_up), :] = g_up[:, j * LANES : (j + 1) * LANES]
 
-    quarter = 4 * shard_rows
-
-    def grad_rows(at):
-        return pl.ds(pl.multiple_of(at * quarter, quarter), quarter)
-
-    g_core_far = send(grad.at[grad_rows(o_diag)], from_core.at[0], core_dev)
-    g_core_own = send(grad.at[grad_rows(o_core)], from_core.at[1], core_dev)
-    arrive(1, 1)
-    pl.when(middle)(lambda: arrive(2, 1))
-    g_core_far.wait_recv()
-    half_sum[0] = grad[grad_rows(o_x), :] + from_core[0]
-    g_x = send(half_sum.at[0], from_x, x_dev)
-    arrive_early(2, 0)
-    g_core_own.wait_recv()
-    half_sum[1] = grad[grad_rows(o), :] + from_core[1]
-    arrive_early(2, 1)
+    part_rows = 2 * shard_rows
+    parts = [pl.ds(p * part_rows, part_rows) for p in range(2)]
+
+    def grad_rows(at, p):
+        return pl.ds(pl.multiple_of((2 * at + p) * part_rows, part_rows), part_rows)
+
+    g_core_far = [
+        send(grad.at[grad_rows(o_diag, p)], from_core.at[0, parts[p]], core_dev) for p in range(2)
+    ]
+    g_core_own = [
+        send(grad.at[grad_rows(o_core, p)], from_core.at[1, parts[p]], core_dev) for p in range(2)
+    ]
     weight_ready(1)
     block_math(1)
-    pl.when(jnp.logical_not(middle))(lambda: arrive(3, 0))
+    block_send(1)
+    g_x = []
+    for p in range(2):
+        g_core_far[p].wait_recv()
+        half_sum[0, parts[p]] = grad[grad_rows(o_x, p), :] + from_core[0, parts[p]]
+        g_x.append(send(half_sum.at[0, parts[p]], from_x.at[parts[p]], x_dev))
+    arrive_early(2, 0)
+    for p in range(2):
+        g_core_own[p].wait_recv()
+        half_sum[1, parts[p]] = grad[grad_rows(o, p), :] + from_core[1, parts[p]]
+    arrive_early(2, 1)
     weight_ready(2)
     block_math(2)
+    pl.when(jnp.logical_not(middle))(lambda: arrive(3, 0))
     pl.when(jnp.logical_not(middle))(lambda: arrive(3, 1))
-    g_x.wait_recv()
-    half_sum[1] += from_x[...]
 
     def shard(at):
         return pl.ds(pl.multiple_of(at * shard_rows, shard_rows), shard_rows)
 
-    g_z = [
-        send(half_sum.at[1, shard(z_to[k])], from_z.at[k - 1], z_devs[k]) for k in range(1, 4)
-    ]
-    block_send(1)
+    def shard_copy(to, source):
+        return pltpu.make_async_remote_copy(
+            src_ref=half_sum.at[1, shard(to)],
+            dst_ref=from_z.at[source],
+            send_sem=shard_send_sem.at[to],
+            recv_sem=shard_recv_sem.at[source],
+            device_id={"inner": to},
+            device_id_type=MESH,
+        )
+
+    for p in range(2):
+        g_x[p].wait_recv()
+        half_sum[1, parts[p]] += from_x[parts[p]]
+        for to in (2 * p, 2 * p + 1):
+            pl.when(z != to)(lambda to=to: shard_copy(to, z).start())
     block_send(2)
     weight_ready(3)
     block_math(3)
     block_send(3)
-    for copy in g_z:
-        copy.wait_recv()
-    total = half_sum[1, shard(z), :] + from_z[0] + from_z[1] + from_z[2]
+    for k in range(1, 4):
+        shard_copy(z_to[k], z_from[k]).wait_recv()
+    total = half_sum[1, shard(z), :]
+    for k in range(1, 4):
+        total += from_z[z_from[k]]
     clipped_ref[...] = total
     sq_own[...] = jnp.sum((total * total).reshape(shard_rows // 8, 8, LANES), axis=0)
     s_z = [send(sq_own, sq_z.at[k - 1], z_devs[k]) for k in range(1, 4)]
@@ -383,6 +405,8 @@
         copy.wait_recv()
     for copy in used:
         copy.wait_send()
+    for k in range(1, 4):
+        shard_copy(z_to[k], z).wait_send()
     for n in range(4):
         for m in range(PIECES):
             b = order[n]
@@ -402,18 +426,29 @@
     new_master_ref,
     new_moment_ref,
     new_second_ref,
-    sem,
+    held,
+    in_sem,
+    out_sem,
 ):
     step = rows_in.shape[0] // ROW_COPIES
-    copies = []
+    cuts = [pl.ds(n * step, step) for n in range(ROW_COPIES)]
+    fetch = [
+        pltpu.make_async_copy(rows_in.at[at], held.at[at], in_sem.at[n])
+        for n, at in enumerate(cuts)
+    ]
+    put = [
+        pltpu.make_async_copy(held.at[at], rows_out.at[at], out_sem.at[n])
+        for n, at in enumerate(cuts)
+    ]
+    for copy in fetch:
+        copy.start()
     for n in range(ROW_COPIES):
-        at = pl.ds(n * step, step)
-        copies.append(pltpu.make_async_copy(rows_in.at[at], rows_out.at[at], sem.at[n]))
-        copies[-1].start()
+        fetch[n].wait()
+        put[n].start()
     new_master_ref[...], new_moment_ref[...], new_second_ref[...] = adam(
         clipped_ref[...], master_ref[...], moment_ref[...], second_ref[...]
     )
-    for copy in copies:
+    for copy in put:
         copy.wait()
 
 
@@ -447,7 +482,7 @@
             pltpu.VMEM((2, 4 * shard_rows, LANES), f32),
             pltpu.VMEM((2, 4 * shard_rows, LANES), f32),
             pltpu.VMEM((4 * shard_rows, LANES), f32),
-            pltpu.VMEM((3, shard_rows, LANES), f32),
+            pltpu.VMEM((4, shard_rows, LANES), f32),
             pltpu.VMEM((8, LANES), f32),
             pltpu.VMEM((3, 8, LANES), f32),
             pltpu.VMEM((8, LANES), f32),
@@ -458,6 +493,8 @@
             pltpu.SemaphoreType.DMA((N_COPIES,)),
             pltpu.SemaphoreType.DMA((3, PIECES, 4)),
             pltpu.SemaphoreType.DMA((2, PIECES, 4)),
+            pltpu.SemaphoreType.DMA((4,)),
+            pltpu.SemaphoreType.DMA((4,)),
         ],
         compiler_params=pltpu.CompilerParams(
             collective_id=0, has_side_effects=True, vmem_limit_bytes=VMEM_GRANT
@@ -469,7 +506,11 @@
         out_shape=(jax.ShapeDtypeStruct((tokens, width), bf16), state, state, state),
         in_specs=[hbm] + [vmem] * 4,
         out_specs=(hbm,) + (vmem,) * 3,
-        scratch_shapes=[pltpu.SemaphoreType.DMA((ROW_COPIES,))],
+        scratch_shapes=[
+            pltpu.VMEM((tokens, width), bf16),
+            pltpu.SemaphoreType.DMA((ROW_COPIES,)),
+            pltpu.SemaphoreType.DMA((ROW_COPIES,)),
+        ],
         compiler_params=pltpu.CompilerParams(vmem_limit_bytes=VMEM_GRANT),
         name="finish",
     )(

time: 131 us -> 81 us (0.62)
  Pallas kernels: 130 us -> 80.1 us
    pallas_call x1, Pallas kernels: 66.6 us -> 4.29 us  [fused(): pl.pallas_call(finish, out_shape=(jax.ShapeDtypeStruct((tokens, width), b...]
    pallas_call x1, Pallas kernels: 63.6 us -> 75.9 us  [fused(): pl.pallas_call(functools.partial(kernel, rank), out_shape=(jax.ShapeDtype...]
where the time goes in v5:
time: 81 us; the launch traced here: 80.8 us
  Pallas kernels  80.1 us (99%)
    pallas_call x1, Pallas kernels, fused(): pl.pallas_call(functools.partial(kernel, rank), out_shape=(jax.ShapeDtype...  75.9 us
    pallas_call x1, Pallas kernels, fused(): pl.pallas_call(finish, out_shape=(jax.ShapeDtypeStruct((tokens, width), b...  4.29 us

profile of v5, /device:TPU:0, one launch (start us, length us, event | category | flops | bytes accessed | tf_op | source)
XLA Modules:
  0.0 80.8 jit_solution(9955719320804895028)
XLA Ops:
  0.6 75.9 %adapter_backward.1 = (bf16[128,8192]{1,0:T(8,128)(2,1)}, f32[280,128]{1,0:T(8,128)}) custom-call(bf16[128,8192]{1,0:T(8,128)(2,1)} %act_hbm.1, bf16[128,768]{1,0:T(8,128)(2,1)} %up_hbm.1, bf16[512,768]{1,0:T(8,128)(2,1)} %w_hbm.1, f32[280,128]{1,0:T(8,128)} %bitcast.6), custom_call_target="tpu_custom_call" | custom-call | tf_op jit(solution)/shard_map/adapter_backward/pallas_call | solution.py:469
  76.5 4.3 %finish.1 = (bf16[128,8192]{1,0:T(8,128)(2,1)}, f32[280,128]{1,0:T(8,128)}, f32[280,128]{1,0:T(8,128)}, f32[280,128]{1,0:T(8,128)}) custom-call(bf16[128,8192]{1,0:T(8,128)(2,1)} %get-tuple-element.10.rows_in, f32[280,128]{1,0:T(8,128)} %get-tuple-element.11.clipped_ref, f32[280,128]{1,0:T(8,128)} %bitcast.7, f32[280,128]{1,0:T(8,128)} %bitcast.8, ...), custom_call_target="tpu_custom_call" | custom-call | tf_op jit(solution)/shard_map/finish/pallas_call | solution.py:504

commit v6 on v5

--- a/solution.py
+++ b/solution.py
@@ -341,9 +341,6 @@
     g_core_own = [
         send(grad.at[grad_rows(o_core, p)], from_core.at[1, parts[p]], core_dev) for p in range(2)
     ]
-    weight_ready(1)
-    block_math(1)
-    block_send(1)
     g_x = []
     for p in range(2):
         g_core_far[p].wait_recv()
@@ -354,10 +351,8 @@
         g_core_own[p].wait_recv()
         half_sum[1, parts[p]] = grad[grad_rows(o, p), :] + from_core[1, parts[p]]
     arrive_early(2, 1)
-    weight_ready(2)
-    block_math(2)
-    pl.when(jnp.logical_not(middle))(lambda: arrive(3, 0))
-    pl.when(jnp.logical_not(middle))(lambda: arrive(3, 1))
+    weight_ready(1)
+    block_math(1)
 
     def shard(at):
         return pl.ds(pl.multiple_of(at * shard_rows, shard_rows), shard_rows)
@@ -377,10 +372,12 @@
         half_sum[1, parts[p]] += from_x[parts[p]]
         for to in (2 * p, 2 * p + 1):
             pl.when(z != to)(lambda to=to: shard_copy(to, z).start())
+    block_send(1)
+    pl.when(jnp.logical_not(middle))(lambda: arrive(3, 0))
+    pl.when(jnp.logical_not(middle))(lambda: arrive(3, 1))
+    weight_ready(2)
+    block_math(2)
     block_send(2)
-    weight_ready(3)
-    block_math(3)
-    block_send(3)
     for k in range(1, 4):
         shard_copy(z_to[k], z_from[k]).wait_recv()
     total = half_sum[1, shard(z), :]
@@ -389,6 +386,9 @@
     clipped_ref[...] = total
     sq_own[...] = jnp.sum((total * total).reshape(shard_rows // 8, 8, LANES), axis=0)
     s_z = [send(sq_own, sq_z.at[k - 1], z_devs[k]) for k in range(1, 4)]
+    weight_ready(3)
+    block_math(3)
+    block_send(3)
     for copy in s_z:
         copy.wait_recv()
     sq_line[...] = sq_own[...] + sq_z[0] + sq_z[1] + sq_z[2]
@@ -416,38 +416,27 @@
                 weight_y(b, m).wait_send()
 
 
-def finish(
-    rows_in,
-    clipped_ref,
-    master_ref,
-    moment_ref,
-    second_ref,
-    rows_out,
-    new_master_ref,
-    new_moment_ref,
-    new_second_ref,
-    held,
-    in_sem,
-    out_sem,
-):
+def finish(rows_in, *refs):
+    states_in, rows_out, states_out = refs[:4], refs[4], refs[5:8]
+    held, held_in, held_out, in_sem, out_sem = refs[8:]
     step = rows_in.shape[0] // ROW_COPIES
     cuts = [pl.ds(n * step, step) for n in range(ROW_COPIES)]
-    fetch = [
-        pltpu.make_async_copy(rows_in.at[at], held.at[at], in_sem.at[n])
-        for n, at in enumerate(cuts)
-    ]
-    put = [
-        pltpu.make_async_copy(held.at[at], rows_out.at[at], out_sem.at[n])
-        for n, at in enumerate(cuts)
-    ]
+    moves = [(rows_in.at[at], held.at[at]) for at in cuts]
+    moves += [(ref, held_in.at[n]) for n, ref in enumerate(states_in)]
+    fetch = [pltpu.make_async_copy(a, b, in_sem.at[n]) for n, (a, b) in enumerate(moves)]
+    moves = [(held.at[at], rows_out.at[at]) for at in cuts]
+    moves += [(held_out.at[n], ref) for n, ref in enumerate(states_out)]
+    put = [pltpu.make_async_copy(a, b, out_sem.at[n]) for n, (a, b) in enumerate(moves)]
     for copy in fetch:
         copy.start()
     for n in range(ROW_COPIES):
         fetch[n].wait()
         put[n].start()
-    new_master_ref[...], new_moment_ref[...], new_second_ref[...] = adam(
-        clipped_ref[...], master_ref[...], moment_ref[...], second_ref[...]
-    )
+    for copy in fetch[ROW_COPIES:]:
+        copy.wait()
+    held_out[0], held_out[1], held_out[2] = adam(*(held_in[n] for n in range(4)))
+    for copy in put[ROW_COPIES:]:
+        copy.start()
     for copy in put:
         copy.wait()
 
@@ -504,12 +493,14 @@
     result = pl.pallas_call(
         finish,
         out_shape=(jax.ShapeDtypeStruct((tokens, width), bf16), state, state, state),
-        in_specs=[hbm] + [vmem] * 4,
-        out_specs=(hbm,) + (vmem,) * 3,
+        in_specs=[hbm] * 5,
+        out_specs=(hbm,) * 4,
         scratch_shapes=[
             pltpu.VMEM((tokens, width), bf16),
-            pltpu.SemaphoreType.DMA((ROW_COPIES,)),
-            pltpu.SemaphoreType.DMA((ROW_COPIES,)),
+            pltpu.VMEM((4, shard_rows, LANES), f32),
+            pltpu.VMEM((3, shard_rows, LANES), f32),
+            pltpu.SemaphoreType.DMA((ROW_COPIES + 4,)),
+            pltpu.SemaphoreType.DMA((ROW_COPIES + 3,)),
         ],
         compiler_params=pltpu.CompilerParams(vmem_limit_bytes=VMEM_GRANT),
         name="finish",

time: 81 us -> 65.7 us (0.81)
  Pallas kernels: 80.1 us -> 65 us
    pallas_call x1, Pallas kernels: 75.9 us -> 62.3 us  [fused(): pl.pallas_call(functools.partial(kernel, rank), out_shape=(jax.ShapeDtype...]
    pallas_call x1, Pallas kernels: 4.29 us -> 2.66 us  [fused(): pl.pallas_call(finish, out_shape=(jax.ShapeDtypeStruct((tokens, width), b...]
where the time goes in v6:
time: 65.7 us; the launch traced here: 65.6 us
  Pallas kernels  65 us (99%)
    pallas_call x1, Pallas kernels, fused(): pl.pallas_call(functools.partial(kernel, rank), out_shape=(jax.ShapeDtype...  62.3 us
    pallas_call x1, Pallas kernels, fused(): pl.pallas_call(finish, out_shape=(jax.ShapeDtypeStruct((tokens, width), b...  2.66 us

profile of v6, /device:TPU:0, one launch (start us, length us, event | category | flops | bytes accessed | tf_op | source)
XLA Modules:
  0.0 65.6 jit_solution(8731094825536319866)
XLA Ops:
  0.6 62.3 %adapter_backward.1 = (bf16[128,8192]{1,0:T(8,128)(2,1)}, f32[280,128]{1,0:T(8,128)}) custom-call(bf16[128,8192]{1,0:T(8,128)(2,1)} %act_hbm.1, bf16[128,768]{1,0:T(8,128)(2,1)} %up_hbm.1, bf16[512,768]{1,0:T(8,128)(2,1)} %w_hbm.1, f32[280,128]{1,0:T(8,128)} %bitcast.6), custom_call_target="tpu_custom_call" | custom-call | tf_op jit(solution)/shard_map/adapter_backward/pallas_call | solution.py:458
  62.9 2.7 %finish.1 = (bf16[128,8192]{1,0:T(8,128)(2,1)}, f32[280,128]{1,0:T(8,128)}, f32[280,128]{1,0:T(8,128)}, f32[280,128]{1,0:T(8,128)}) custom-call(bf16[128,8192]{1,0:T(8,128)(2,1)} %get-tuple-element.10.rows_in, f32[280,128]{1,0:T(8,128)} %get-tuple-element.11.refs_0_, f32[280,128]{1,0:T(8,128)} %bitcast.7, f32[280,128]{1,0:T(8,128)} %bitcast.8, ...), custom_call_target="tpu_custom_call" | custom-call | tf_op jit(solution)/shard_map/finish/pallas_call | solution.py:493

commit v7 on v6

--- a/solution.py
+++ b/solution.py
@@ -287,24 +287,32 @@
 
     block_copies = []
 
-    def block_cols(n):
-        return pl.ds(pl.multiple_of((o * 4 + order[n]) * feats, feats), feats)
-
-    def block_math(n):
-        cols = block_cols(n)
-        per_block = feats // LANES
-        d_block = down_part((o * 4 + order[n]) * per_block, per_block)
-        value = dot(up_all[...].reshape(u_rows, value_width), w_buf[order[n]], (1, 1))
+    def block_cols(n, h):
+        at = (o * 4 + order[n]) * 2 + (y if h == 0 else 1 - y)
+        return pl.ds(pl.multiple_of(at * half, half), half)
+
+    def block_math(n, h):
+        side = y if h == 0 else 1 - y
+        per_block = half // LANES
+        d_block = down_part(((o * 4 + order[n]) * 2 + side) * per_block, per_block)
+        w = w_buf[order[n], pl.ds(pl.multiple_of(side * half, half), half), :]
+        value = dot(up_all[...].reshape(u_rows, value_width), w, (1, 1))
         value += scale * dot(rank_all, d_block, (1, 0))
-        blocks[n] = value.astype(jnp.bfloat16).reshape(4, tokens, feats)
-        out_ref[:, cols] = blocks[n, o]
-
-    def block_send(n):
+        blocks[n, h] = value.astype(jnp.bfloat16).reshape(4, tokens, half)
+        out_ref[:, block_cols(n, h)] = blocks[n, h, o]
+
+    def block_send(n, h):
         for to, device in ((o_x, x_dev), (o_diag, diag_dev), (o_core, core_dev)):
-            block_copies.append(send(blocks.at[n, to], out_ref.at[:, block_cols(n)], device))
-
-    block_math(0)
-    block_send(0)
+            block_copies.append(
+                send(blocks.at[n, h, to], out_ref.at[:, block_cols(n, h)], device)
+            )
+
+    def block(n, h):
+        block_math(n, h)
+        block_send(n, h)
+
+    block(0, 0)
+    block(0, 1)
     arrive(1, 0)
     pl.when(middle)(lambda: arrive(2, 0))
 
@@ -351,8 +359,9 @@
         g_core_own[p].wait_recv()
         half_sum[1, parts[p]] = grad[grad_rows(o, p), :] + from_core[1, parts[p]]
     arrive_early(2, 1)
+    block_math(1, 0)
     weight_ready(1)
-    block_math(1)
+    block_math(1, 1)
 
     def shard(at):
         return pl.ds(pl.multiple_of(at * shard_rows, shard_rows), shard_rows)
@@ -372,12 +381,15 @@
         half_sum[1, parts[p]] += from_x[parts[p]]
         for to in (2 * p, 2 * p + 1):
             pl.when(z != to)(lambda to=to: shard_copy(to, z).start())
-    block_send(1)
-    pl.when(jnp.logical_not(middle))(lambda: arrive(3, 0))
+        if p == 0:
+            pl.when(jnp.logical_not(middle))(lambda: arrive(3, 0))
+    block_send(1, 0)
+    block_send(1, 1)
     pl.when(jnp.logical_not(middle))(lambda: arrive(3, 1))
+    block(2, 0)
     weight_ready(2)
-    block_math(2)
-    block_send(2)
+    block(2, 1)
+    block(3, 0)
     for k in range(1, 4):
         shard_copy(z_to[k], z_from[k]).wait_recv()
     total = half_sum[1, shard(z), :]
@@ -387,8 +399,7 @@
     sq_own[...] = jnp.sum((total * total).reshape(shard_rows // 8, 8, LANES), axis=0)
     s_z = [send(sq_own, sq_z.at[k - 1], z_devs[k]) for k in range(1, 4)]
     weight_ready(3)
-    block_math(3)
-    block_send(3)
+    block(3, 1)
     for copy in s_z:
         copy.wait_recv()
     sq_line[...] = sq_own[...] + sq_z[0] + sq_z[1] + sq_z[2]
@@ -476,7 +487,7 @@
             pltpu.VMEM((3, 8, LANES), f32),
             pltpu.VMEM((8, LANES), f32),
             pltpu.VMEM((3, 8, LANES), f32),
-            pltpu.VMEM((4, 4, tokens, feats), bf16),
+            pltpu.VMEM((4, 2, 4, tokens, feats // 2), bf16),
             pltpu.SemaphoreType.DMA((4,)),
             pltpu.SemaphoreType.DMA((N_COPIES,)),
             pltpu.SemaphoreType.DMA((N_COPIES,)),

time: 65.7 us -> 65.6 us (level)
  no operation moved by 1% of the time
where the time goes in v7:
time: 65.6 us; the launch traced here: 65.4 us
  Pallas kernels  64.8 us (99%)
    pallas_call x1, Pallas kernels, fused(): pl.pallas_call(functools.partial(kernel, rank), out_shape=(jax.ShapeDtype...  62.1 us
    pallas_call x1, Pallas kernels, fused(): pl.pallas_call(finish, out_shape=(jax.ShapeDtypeStruct((tokens, width), b...  2.66 us

profile of v7, /device:TPU:0, one launch (start us, length us, event | category | flops | bytes accessed | tf_op | source)
XLA Modules:
  0.0 65.4 jit_solution(11296375909548877198)
XLA Ops:
  0.6 62.1 %adapter_backward.1 = (bf16[128,8192]{1,0:T(8,128)(2,1)}, f32[280,128]{1,0:T(8,128)}) custom-call(bf16[128,8192]{1,0:T(8,128)(2,1)} %act_hbm.1, bf16[128,768]{1,0:T(8,128)(2,1)} %up_hbm.1, bf16[512,768]{1,0:T(8,128)(2,1)} %w_hbm.1, f32[280,128]{1,0:T(8,128)} %bitcast.6), custom_call_target="tpu_custom_call" | custom-call | tf_op jit(solution)/shard_map/adapter_backward/pallas_call | solution.py:469
  62.7 2.7 %finish.1 = (bf16[128,8192]{1,0:T(8,128)(2,1)}, f32[280,128]{1,0:T(8,128)}, f32[280,128]{1,0:T(8,128)}, f32[280,128]{1,0:T(8,128)}) custom-call(bf16[128,8192]{1,0:T(8,128)(2,1)} %get-tuple-element.10.rows_in, f32[280,128]{1,0:T(8,128)} %get-tuple-element.11.refs_0_, f32[280,128]{1,0:T(8,128)} %bitcast.7, f32[280,128]{1,0:T(8,128)} %bitcast.8, ...), custom_call_target="tpu_custom_call" | custom-call | tf_op jit(solution)/shard_map/finish/pallas_call | solution.py:504

commit v8 on v7

--- a/solution.py
+++ b/solution.py
@@ -245,9 +245,6 @@
     slot_z = [None] + [send(slots.at[own], slots.at[own], z_devs[k]) for k in range(1, 4)]
     slot_x = [send(slots.at[own], slots.at[own], x_dev)]
     slot_core = [send(slots.at[own], slots.at[own], core_dev)]
-    load_up.wait()
-    u_x = send(up_all.at[o], up_all.at[o], x_dev)
-    u_core = send(up_all.at[o], up_all.at[o], core_dev)
     for k in range(1, 4):
         slot_z[k].wait_recv()
         at = slots.at[o * 4 + z_from[k]]
@@ -256,14 +253,15 @@
     load_w.wait()
     for m in range(PIECES):
         pass_on(z, m)
+    load_up.wait()
+    u_x = send(up_all.at[o], up_all.at[o], x_dev)
+    u_core = send(up_all.at[o], up_all.at[o], core_dev)
     for k in range(4):
         to_flat(o * 4 + z_from[k])
     for k in range(4):
         slot_x[k].wait_recv()
         at = slots.at[o_x * 4 + z_from[k]]
         slot_core.append(send(at, at, core_dev))
-    u_x.wait_recv()
-    u_far = send(up_all.at[o_x], up_all.at[o_x], core_dev)
     for k in range(4):
         to_flat(o_x * 4 + z_from[k])
     for k in range(8):
@@ -280,6 +278,41 @@
         rows = [flat[pl.ds(first + j, rank, stride=per_row), :] for j in range(count)]
         return jnp.concatenate(rows, axis=1).astype(jnp.bfloat16)
 
+    own_rank_t = jnp.transpose(dot(up_all[o], up_m, (1, 1))).astype(jnp.bfloat16)
+    load_act.wait()
+
+    def part(n, projected):
+        cols = pl.ds(pl.multiple_of(n * CHUNK, CHUNK), CHUNK)
+        a_part = act_ref[:, cols]
+        g_part = scale * dot(own_rank_t, a_part, (1, 0))
+        for j in range(CHUNK // LANES):
+            at = pl.ds(n * (CHUNK // LANES) + j, rank, stride=per_row)
+            grad[at, :] = g_part[:, j * LANES : (j + 1) * LANES]
+        return projected + dot(a_part, down_part(n * (CHUNK // LANES), CHUNK // LANES), (1, 1))
+
+    projected = lax.fori_loop(
+        0, width // CHUNK, part, jnp.zeros((tokens, rank), jnp.float32)
+    ).astype(jnp.bfloat16)
+    u_x.wait_recv()
+    u_far = send(up_all.at[o_x], up_all.at[o_x], core_dev)
+    arrive(1, 0)
+    pl.when(middle)(lambda: arrive(2, 0))
+    g_up = scale * dot(projected, up_all[o], (0, 0))
+    for j in range(per_up):
+        grad[pl.ds(down_rows + j, rank, stride=per_up), :] = g_up[:, j * LANES : (j + 1) * LANES]
+
+    part_rows = 2 * shard_rows
+    parts = [pl.ds(p * part_rows, part_rows) for p in range(2)]
+
+    def grad_rows(at, p):
+        return pl.ds(pl.multiple_of((2 * at + p) * part_rows, part_rows), part_rows)
+
+    g_core_far = [
+        send(grad.at[grad_rows(o_diag, p)], from_core.at[0, parts[p]], core_dev) for p in range(2)
+    ]
+    g_core_own = [
+        send(grad.at[grad_rows(o_core, p)], from_core.at[1, parts[p]], core_dev) for p in range(2)
+    ]
     u_core.wait_recv()
     u_far.wait_recv()
     u_rows = 4 * tokens
@@ -313,47 +346,13 @@
 
     block(0, 0)
     block(0, 1)
-    arrive(1, 0)
-    pl.when(middle)(lambda: arrive(2, 0))
-
-    own_rank_t = jnp.transpose(dot(up_all[o], up_m, (1, 1))).astype(jnp.bfloat16)
-    load_act.wait()
-
-    def part(n, projected):
-        cols = pl.ds(pl.multiple_of(n * CHUNK, CHUNK), CHUNK)
-        a_part = act_ref[:, cols]
-        g_part = scale * dot(own_rank_t, a_part, (1, 0))
-        for j in range(CHUNK // LANES):
-            at = pl.ds(n * (CHUNK // LANES) + j, rank, stride=per_row)
-            grad[at, :] = g_part[:, j * LANES : (j + 1) * LANES]
-        return projected + dot(a_part, down_part(n * (CHUNK // LANES), CHUNK // LANES), (1, 1))
-
-    projected = lax.fori_loop(
-        0, width // CHUNK, part, jnp.zeros((tokens, rank), jnp.float32)
-    ).astype(jnp.bfloat16)
-    arrive(1, 1)
-    pl.when(middle)(lambda: arrive(2, 1))
-    g_up = scale * dot(projected, up_all[o], (0, 0))
-    for j in range(per_up):
-        grad[pl.ds(down_rows + j, rank, stride=per_up), :] = g_up[:, j * LANES : (j + 1) * LANES]
-
-    part_rows = 2 * shard_rows
-    parts = [pl.ds(p * part_rows, part_rows) for p in range(2)]
-
-    def grad_rows(at, p):
-        return pl.ds(pl.multiple_of((2 * at + p) * part_rows, part_rows), part_rows)
-
-    g_core_far = [
-        send(grad.at[grad_rows(o_diag, p)], from_core.at[0, parts[p]], core_dev) for p in range(2)
-    ]
-    g_core_own = [
-        send(grad.at[grad_rows(o_core, p)], from_core.at[1, parts[p]], core_dev) for p in range(2)
-    ]
     g_x = []
     for p in range(2):
         g_core_far[p].wait_recv()
         half_sum[0, parts[p]] = grad[grad_rows(o_x, p), :] + from_core[0, parts[p]]
         g_x.append(send(half_sum.at[0, parts[p]], from_x.at[parts[p]], x_dev))
+    arrive(1, 1)
+    pl.when(middle)(lambda: arrive(2, 1))
     arrive_early(2, 0)
     for p in range(2):
         g_core_own[p].wait_recv()

time: 65.6 us -> 69.5 us (1.059)
  Pallas kernels: 64.8 us -> 68.7 us
    pallas_call x1, Pallas kernels: 62.1 us -> 66.1 us  [fused(): pl.pallas_call(functools.partial(kernel, rank), out_shape=(jax.ShapeDtype...]
where the time goes in v8:
time: 69.5 us; the launch traced here: 69.4 us
  Pallas kernels  68.7 us (99%)
    pallas_call x1, Pallas kernels, fused(): pl.pallas_call(functools.partial(kernel, rank), out_shape=(jax.ShapeDtype...  66.1 us
    pallas_call x1, Pallas kernels, fused(): pl.pallas_call(finish, out_shape=(jax.ShapeDtypeStruct((tokens, width), b...  2.66 us

profile of v8, /device:TPU:0, one launch (start us, length us, event | category | flops | bytes accessed | tf_op | source)
XLA Modules:
  0.0 69.4 jit_solution(17944973775697466648)
XLA Ops:
  0.6 66.1 %adapter_backward.1 = (bf16[128,8192]{1,0:T(8,128)(2,1)}, f32[280,128]{1,0:T(8,128)}) custom-call(bf16[128,8192]{1,0:T(8,128)(2,1)} %act_hbm.1, bf16[128,768]{1,0:T(8,128)(2,1)} %up_hbm.1, bf16[512,768]{1,0:T(8,128)(2,1)} %w_hbm.1, f32[280,128]{1,0:T(8,128)} %bitcast.6), custom_call_target="tpu_custom_call" | custom-call | tf_op jit(solution)/shard_map/adapter_backward/pallas_call | solution.py:468
  66.7 2.7 %finish.1 = (bf16[128,8192]{1,0:T(8,128)(2,1)}, f32[280,128]{1,0:T(8,128)}, f32[280,128]{1,0:T(8,128)}, f32[280,128]{1,0:T(8,128)}) custom-call(bf16[128,8192]{1,0:T(8,128)(2,1)} %get-tuple-element.10.rows_in, f32[280,128]{1,0:T(8,128)} %get-tuple-element.11.refs_0_, f32[280,128]{1,0:T(8,128)} %bitcast.7, f32[280,128]{1,0:T(8,128)} %bitcast.8, ...), custom_call_target="tpu_custom_call" | custom-call | tf_op jit(solution)/shard_map/finish/pallas_call | solution.py:503

commit v9 on v7

--- a/solution.py
+++ b/solution.py
@@ -248,13 +248,14 @@
     load_up.wait()
     u_x = send(up_all.at[o], up_all.at[o], x_dev)
     u_core = send(up_all.at[o], up_all.at[o], core_dev)
+    load_w.wait()
+    pass_on(z, 0)
     for k in range(1, 4):
         slot_z[k].wait_recv()
         at = slots.at[o * 4 + z_from[k]]
         slot_x.append(send(at, at, x_dev))
         slot_core.append(send(at, at, core_dev))
-    load_w.wait()
-    for m in range(PIECES):
+    for m in range(1, PIECES):
         pass_on(z, m)
     for k in range(4):
         to_flat(o * 4 + z_from[k])
@@ -311,10 +312,12 @@
         block_math(n, h)
         block_send(n, h)
 
+    arrive(1, 0)
+    pl.when(middle)(lambda: arrive(2, 0))
     block(0, 0)
     block(0, 1)
-    arrive(1, 0)
-    pl.when(middle)(lambda: arrive(2, 0))
+    arrive(1, 1)
+    pl.when(middle)(lambda: arrive(2, 1))
 
     own_rank_t = jnp.transpose(dot(up_all[o], up_m, (1, 1))).astype(jnp.bfloat16)
     load_act.wait()
@@ -331,8 +334,6 @@
     projected = lax.fori_loop(
         0, width // CHUNK, part, jnp.zeros((tokens, rank), jnp.float32)
     ).astype(jnp.bfloat16)
-    arrive(1, 1)
-    pl.when(middle)(lambda: arrive(2, 1))
     g_up = scale * dot(projected, up_all[o], (0, 0))
     for j in range(per_up):
         grad[pl.ds(down_rows + j, rank, stride=per_up), :] = g_up[:, j * LANES : (j + 1) * LANES]
@@ -349,12 +350,12 @@
     g_core_own = [
         send(grad.at[grad_rows(o_core, p)], from_core.at[1, parts[p]], core_dev) for p in range(2)
     ]
+    arrive_early(2, 0)
     g_x = []
     for p in range(2):
         g_core_far[p].wait_recv()
         half_sum[0, parts[p]] = grad[grad_rows(o_x, p), :] + from_core[0, parts[p]]
         g_x.append(send(half_sum.at[0, parts[p]], from_x.at[parts[p]], x_dev))
-    arrive_early(2, 0)
     for p in range(2):
         g_core_own[p].wait_recv()
         half_sum[1, parts[p]] = grad[grad_rows(o, p), :] + from_core[1, parts[p]]

time: 65.6 us -> 66.4 us (1.012)
  Pallas kernels: 64.8 us -> 65.6 us
    pallas_call x1, Pallas kernels: 62.1 us -> 62.9 us  [fused(): pl.pallas_call(functools.partial(kernel, rank), out_shape=(jax.ShapeDtype...]
where the time goes in v9:
time: 66.4 us; the launch traced here: 66.2 us
  Pallas kernels  65.6 us (99%)
    pallas_call x1, Pallas kernels, fused(): pl.pallas_call(functools.partial(kernel, rank), out_shape=(jax.ShapeDtype...  62.9 us
    pallas_call x1, Pallas kernels, fused(): pl.pallas_call(finish, out_shape=(jax.ShapeDtypeStruct((tokens, width), b...  2.66 us

profile of v9, /device:TPU:0, one launch (start us, length us, event | category | flops | bytes accessed | tf_op | source)
XLA Modules:
  0.0 66.2 jit_solution(11225226656869775526)
XLA Ops:
  0.6 62.9 %adapter_backward.1 = (bf16[128,8192]{1,0:T(8,128)(2,1)}, f32[280,128]{1,0:T(8,128)}) custom-call(bf16[128,8192]{1,0:T(8,128)(2,1)} %act_hbm.1, bf16[128,768]{1,0:T(8,128)(2,1)} %up_hbm.1, bf16[512,768]{1,0:T(8,128)(2,1)} %w_hbm.1, f32[280,128]{1,0:T(8,128)} %bitcast.6), custom_call_target="tpu_custom_call" | custom-call | tf_op jit(solution)/shard_map/adapter_backward/pallas_call | solution.py:470
  63.6 2.7 %finish.1 = (bf16[128,8192]{1,0:T(8,128)(2,1)}, f32[280,128]{1,0:T(8,128)}, f32[280,128]{1,0:T(8,128)}, f32[280,128]{1,0:T(8,128)}) custom-call(bf16[128,8192]{1,0:T(8,128)(2,1)} %get-tuple-element.10.rows_in, f32[280,128]{1,0:T(8,128)} %get-tuple-element.11.refs_0_, f32[280,128]{1,0:T(8,128)} %bitcast.7, f32[280,128]{1,0:T(8,128)} %bitcast.8, ...), custom_call_target="tpu_custom_call" | custom-call | tf_op jit(solution)/shard_map/finish/pallas_call | solution.py:505
